TPU v7x, 32 devices: a whole 2x2x4 slice. The times are simulated.
32 devices in a mesh: section: 4 (over x, core), seq: 8 (over z, y).
Axes of the slice: x: 2, y: 2, z: 4, core: 2. Of those that a mesh axis runs over, the one named last changes fastest.
Arguments:
- residual: bfloat16 [4, 2048, 2048], P('section', 'seq'), may hold values from -6 to 6
- w_qkv: bfloat16 [4, 2048, 6144], P('section', 'seq'), may hold values from -0.125 to 0.125
- w_beta: bfloat16 [4, 2048, 16], P('section', 'seq'), may hold values from -0.125 to 0.125
- beta_bias: float32 [4, 16], P('section'), may hold values from -8 to 2
- norm_gain: float32 [4, 2048], P('section'), may hold values from 0.1 to 1.9
- out_gain: float32 [4, 128], P('section'), may hold values from 0.1 to 1.9
- state_in: float32 [4, 16, 128, 128], P('section'), may hold values from -6 to 6
- doc_start: int32 [2, 4], P(None, 'section'), may hold values from 0 to 32, as said below
Outputs:
- stream_out: bfloat16 [4, 2048, 2048], P('section', 'seq')
Inputs may be any that keep to these rules, and one draw needn't show every extreme that they name: `doc_start`: 32 means no new document in that micro-batch.
All inputs are finite; a program needn't handle non-finite values.
Results may differ from a plain program's by a relative error of at most 0.03.
Values may be sent and summed in bfloat16 or wider, within the bound.
A program may use at most 192 MiB of HBM per device.

v0:
```python
import jax
import jax.numpy as jnp
from jax import lax
from jax.sharding import PartitionSpec as P

HEADS = 16
HD = 128
GROUP = 64
TICKS = 2


FULL_PRECISION = lax.Precision.HIGHEST


def from_behind(value, axis, by):
    count = lax.axis_size(axis)
    pairs = [(i, i + by) for i in range(count) if 0 <= i + by < count]
    return lax.ppermute(value, axis, pairs)


def from_root(value, axis, source):
    kept = jnp.where(lax.axis_index(axis) == source, value, 0).astype(value.dtype)
    return lax.psum(kept, axis)


def passed_along(value, axis, by):
    count = lax.axis_size(axis)
    return lax.ppermute(value, axis, [(i, (i + by) % count) for i in range(count)])


def unit_norm(projected):
    return projected * lax.rsqrt(jnp.sum(projected * projected, axis=-1, keepdims=True) + 1e-06)


def block_solve(key_rows, values, beta_rows):
    block_len = key_rows.shape[-2]
    intersections = jnp.einsum("ghik,ghjk->ghij", key_rows, key_rows, precision=FULL_PRECISION)
    system = jnp.tril(intersections * beta_rows[..., :, None], -1) + jnp.eye(
        block_len, dtype=jnp.float32
    )
    right_side = jnp.concatenate(
        [values * beta_rows[..., None], key_rows * beta_rows[..., None]], axis=-1
    )
    solved = lax.linalg.triangular_solve(
        system, right_side, left_side=True, lower=True, unit_diagonal=True
    )
    head_width = values.shape[-1]
    return (solved[..., :head_width], solved[..., head_width:])


def prepare(stream, weight_qkv, weight_beta, head_bias, in_gain):
    row_count = stream.shape[0]
    widened = stream.astype(jnp.float32)
    normed = (
        widened * lax.rsqrt(jnp.mean(widened * widened, axis=-1, keepdims=True) + 1e-05) * in_gain
    ).astype(jnp.bfloat16)
    projected = jnp.dot(normed, weight_qkv, preferred_element_type=jnp.float32).reshape(
        row_count, 3, HEADS, HD
    )
    queries = unit_norm(projected[:, 0]).astype(jnp.bfloat16)
    key_rows = unit_norm(projected[:, 1]).astype(jnp.bfloat16)
    values = projected[:, 2].astype(jnp.bfloat16)
    beta_rows = jax.nn.sigmoid(
        jnp.dot(normed, weight_beta, preferred_element_type=jnp.float32) + head_bias
    )
    blocks = row_count // GROUP

    def to_blocks(tensor):
        return tensor.astype(jnp.float32).reshape(blocks, GROUP, HEADS, HD).transpose(0, 2, 1, 3)

    beta_blk = beta_rows.reshape(blocks, GROUP, HEADS).transpose(0, 2, 1)
    key_block = to_blocks(key_rows)
    inject, weights = block_solve(key_block, to_blocks(values), beta_blk)
    return (to_blocks(queries), key_block, inject, weights, widened)


def run_blocks(queries, key_rows, inject, weights, current_state, doc_block, first_block):
    block_count = queries.shape[0]
    block_len = queries.shape[2]
    causal = jnp.tril(jnp.ones((block_len, block_len), jnp.float32))

    def run_advance(current_state, pieces):
        query_block, key_block, inject_block, weight_block, block_index = pieces
        current_state = jnp.where(
            block_index == doc_block, jnp.zeros_like(current_state), current_state
        )
        delta_values = inject_block - jnp.einsum(
            "jxy,jyu->jxu", weight_block, current_state, precision=FULL_PRECISION
        )
        attention_scores = (
            jnp.einsum("hik,hjk->hij", query_block, key_block, precision=FULL_PRECISION) * causal
        )
        block_result = jnp.einsum(
            "jxy,jyu->jxu", query_block, current_state, precision=FULL_PRECISION
        ) + jnp.einsum("ucd,udo->uco", attention_scores, delta_values, precision=FULL_PRECISION)
        current_state = current_state + jnp.einsum(
            "plq,plw->pqw", key_block, delta_values, precision=FULL_PRECISION
        )
        return (current_state, block_result)

    block_ids = first_block + jnp.arange(block_count, dtype=jnp.int32)
    return lax.scan(run_advance, current_state, (queries, key_rows, inject, weights, block_ids))


def transitions(key_rows, inject, weights, doc_block, first_block):
    head_count = key_rows.shape[1]
    head_width = key_rows.shape[3]
    block_count = key_rows.shape[0]
    identity = jnp.broadcast_to(
        jnp.eye(head_width, dtype=jnp.float32), (head_count, head_width, head_width)
    )

    def transitions_advance(maps, pieces):
        decay_matrix, start_offset = maps
        key_block, inject_block, weight_block, block_index = pieces
        keep_flag = block_index != doc_block
        decay_matrix = jnp.where(keep_flag, decay_matrix, jnp.zeros_like(decay_matrix))
        start_offset = jnp.where(keep_flag, start_offset, jnp.zeros_like(start_offset))
        decay_matrix = decay_matrix - jnp.einsum(
            "plq,plw->pqw",
            key_block,
            jnp.einsum("jxy,jyu->jxu", weight_block, decay_matrix, precision=FULL_PRECISION),
            precision=FULL_PRECISION,
        )
        start_offset = start_offset + jnp.einsum(
            "plq,plw->pqw",
            key_block,
            inject_block
            - jnp.einsum("jxy,jyu->jxu", weight_block, start_offset, precision=FULL_PRECISION),
            precision=FULL_PRECISION,
        )
        return ((decay_matrix, start_offset), None)

    block_ids = first_block + jnp.arange(block_count, dtype=jnp.int32)
    maps, unused = lax.scan(
        transitions_advance,
        (identity, jnp.zeros_like(identity)),
        (key_rows, inject, weights, block_ids),
    )
    return maps


def apply_map(maps, given_state):
    return jnp.einsum("hij,hjk->hik", maps[0], given_state, precision=FULL_PRECISION) + maps[1]


def compose(earlier, latter):
    return (
        jnp.einsum("hij,hjk->hik", latter[0], earlier[0], precision=FULL_PRECISION),
        jnp.einsum("hij,hjk->hik", latter[0], earlier[1], precision=FULL_PRECISION) + latter[1],
    )


def finish(widened, block_result, head_gain):
    blocks = block_result.shape[0]
    mixed = block_result.transpose(0, 2, 1, 3).reshape(blocks * GROUP, HEADS, HD)
    mixed = mixed * lax.rsqrt(jnp.mean(mixed * mixed, axis=-1, keepdims=True) + 1e-05) * head_gain
    return (widened + mixed.reshape(blocks * GROUP, HEADS * HD)).astype(jnp.bfloat16)


def shards(residual, w_qkv, w_beta, beta_bias, norm_gain, out_gain, state_in, doc_start):
    weight_qkv, weight_beta = (
        lax.all_gather(w_qkv[0], "seq", axis=0, tiled=True),
        lax.all_gather(w_beta[0], "seq", axis=0, tiled=True),
    )
    seq_count = lax.axis_size("seq")
    position = lax.axis_index("seq")
    stream = residual[0]
    given_state = state_in[0]
    blocks = stream.shape[0] // GROUP
    first_block = position * blocks
    outputs = stream
    identity = jnp.broadcast_to(jnp.eye(HD, dtype=jnp.float32), (HEADS, HD, HD))
    empty_map = jnp.stack([identity, jnp.zeros_like(identity)])
    for tick_index in range(TICKS):
        doc_block = doc_start[tick_index, 0]
        queries, key_rows, inject, weights, widened = prepare(
            stream, weight_qkv, weight_beta, beta_bias[0], norm_gain[0]
        )
        maps = transitions(key_rows, inject, weights, doc_block, first_block)

        def hop_once(hop_index, carried_map):
            joined = compose((carried_map[0], carried_map[1]), maps)
            passed = from_behind(
                jnp.stack([joined[0], joined[1]]).astype(jnp.bfloat16), "seq", 1
            ).astype(jnp.float32)
            return jnp.where(position == 0, empty_map, passed)

        prefix_map = lax.fori_loop(0, seq_count - 1, hop_once, empty_map)
        prefix = (prefix_map[0], prefix_map[1])
        entry_state = apply_map(prefix, given_state)
        final_state, block_result = run_blocks(
            queries, key_rows, inject, weights, entry_state, doc_block, first_block
        )
        outputs = finish(widened, block_result, out_gain[0])
        if tick_index + 1 < TICKS:
            given_state = from_root(final_state.astype(jnp.bfloat16), "seq", seq_count - 1).astype(
                final_state.dtype
            )
            stream = passed_along(outputs, "section", 1)
    return outputs[None]


def solution(mesh):
    return jax.shard_map(
        shards,
        mesh=mesh,
        in_specs=(
            P("section", "seq", None),
            P("section", "seq", None),
            P("section", "seq", None),
            P("section", None),
            P("section", None),
            P("section", None),
            P("section", None, None, None),
            P(None, "section"),
        ),
        out_specs=P("section", "seq", None),
        check_vma=False,
    )
```

profile of v0, /device:TPU:28, one launch (start us, length us, event | category | flops | bytes accessed | tf_op | source)
XLA Modules:
  0.0 1936.3 jit_solution(3609424295919207558)
XLA Ops:
  7.4 63.6 %all-gather.1 = bf16[1,2048,16]{1,2,0:T(8,128)(2,1)S(1)} all-gather(bf16[1,256,16]{1,2,0:T(8,128)(2,1)S(1)} %copy-done.19), channel_id=3, replica_groups=mesh['section'=4,'seq'=8] {'seq'}, dimensions={1}, use_global_device_ids=true | all-gather | bytes 73728 | tf_op jit(solution)/shard_map/all_gather | solution.py:164
  74.9 415.1 %all-gather.4.cloned.1.call-done = bf16[1,2048,6144]{2,1,0:T(8,128)(2,1)} async-done(((bf16[1,256,6144]{2,1,0:T(8,128)(2,1)}), bf16[1,2048,6144]{2,1,0:T(8,128)(2,1)}) %all-gather.4.cloned.1.call-update) | async-done | bytes 25165840 | tf_op jit(solution)/shard_map/all_gather | solution.py:163
  490.0 32.3 %copy.95 = bf16[6144,2048]{1,0:T(8,128)(2,1)} copy(bf16[6144,2048]{0,1:T(8,128)(2,1)} %bitcast.357) | data formatting | bytes 50331648 | tf_op jit(solution)/shard_map/dot_general | solution.py:57
  522.3 11.4 fusion.150
  536.6 3.9 broadcast_multiply_fusion.1
  544.6 316.0 %custom-call.6 = f32[4,16,1,64,64]{3,4,2,1,0:T(8,128)} custom-call(f32[4,16,1,64,64]{4,3,2,1,0:T(8,128)} %add_bitcast_fusion.1), custom_call_target="InvertDiagBlocksLowerTriangular" | custom-call | tf_op jit(solution)/shard_map/triangular_solve/custom-call.1 | solution.py:44
  860.5 6.6 fusion.107
  869.9 41.1 %while.80 = (s32[]{:T(128)}, f32[16,128,128]{2,1,0:T(8,128)S(1)}, f32[16,128,128]{2,1,0:T(8,128)S(1)}, s32[4]{0:T(128)S(1)}, s32[]{:T(128)}, /*index=5*/f32[4,16...) while((s32[]{:T(128)}, f32[16,128,128]{2,1,0:T(8,128)S(1)}, ...), condition=%wide.region_3.5_spmd.clone, body=%wide.region_2.4_spmd.clone.sunk | while | flops 807534592 | bytes 19400364 | solution.py:135
  911.1 232.2 %while.76 = (s32[]{:T(128)}, f32[2,16,128,128]{3,2,1,0:T(8,128)}, pred[]{:T(512)}, f32[16,128,128]{2,1,0:T(8,128)S(1)}, f32[16,128,128]{2,1,0:T(8,128)S(1)}, /*index=5*/f32[2,16,128,128]{3,2,1,0:T(8,128)}, s32[]{:T(128)}) while((s32[]{:T(128)}, f32[2,16,128,128]{3,2,1,0:T(8,128)}, pred[]{:T(512)}, f32[16,128,128]{2,1,0:T(8,128)S(1)}, ...), condition=%wide.region_5.7_spmd, body=%wide.region_4.6_spmd.sunk | while | flops 807665664 | bytes 26214544 | solution.py:189
  917.2 26.0 %collective-permute-done = bf16[2,16,128,128]{3,2,1,0:T(8,128)(2,1)} collective-permute-done((bf16[2,16,128,128]{3,2,1,0:T(8,128)(2,1)}, bf16[2,16,128,128]{3,2,1,0:T(8,128)(2,1)}, u32[]{:S(2)}, u32[]{:S(2)}) %collective-permute-start) | collective-permute-done | bytes 1048608 | tf_op jit(solution)/shard_map/while/body/eval_jaxpr/ppermute | solution.py:18
  952.3 26.0 %collective-permute-done = bf16[2,16,128,128]{3,2,1,0:T(8,128)(2,1)} collective-permute-done((bf16[2,16,128,128]{3,2,1,0:T(8,128)(2,1)}, bf16[2,16,128,128]{3,2,1,0:T(8,128)(2,1)}, u32[]{:S(2)}, u32[]{:S(2)}) %collective-permute-start) | collective-permute-done | bytes 1048608 | tf_op jit(solution)/shard_map/while/body/eval_jaxpr/ppermute | solution.py:18
  987.4 25.2 %collective-permute-done = bf16[2,16,128,128]{3,2,1,0:T(8,128)(2,1)} collective-permute-done((bf16[2,16,128,128]{3,2,1,0:T(8,128)(2,1)}, bf16[2,16,128,128]{3,2,1,0:T(8,128)(2,1)}, u32[]{:S(2)}, u32[]{:S(2)}) %collective-permute-start) | collective-permute-done | bytes 1048608 | tf_op jit(solution)/shard_map/while/body/eval_jaxpr/ppermute | solution.py:18
  1021.6 24.3 %collective-permute-done = bf16[2,16,128,128]{3,2,1,0:T(8,128)(2,1)} collective-permute-done((bf16[2,16,128,128]{3,2,1,0:T(8,128)(2,1)}, bf16[2,16,128,128]{3,2,1,0:T(8,128)(2,1)}, u32[]{:S(2)}, u32[]{:S(2)}) %collective-permute-start) | collective-permute-done | bytes 1048608 | tf_op jit(solution)/shard_map/while/body/eval_jaxpr/ppermute | solution.py:18
  1055.0 23.3 %collective-permute-done = bf16[2,16,128,128]{3,2,1,0:T(8,128)(2,1)} collective-permute-done((bf16[2,16,128,128]{3,2,1,0:T(8,128)(2,1)}, bf16[2,16,128,128]{3,2,1,0:T(8,128)(2,1)}, u32[]{:S(2)}, u32[]{:S(2)}) %collective-permute-start) | collective-permute-done | bytes 1048608 | tf_op jit(solution)/shard_map/while/body/eval_jaxpr/ppermute | solution.py:18
  1087.4 22.4 %collective-permute-done = bf16[2,16,128,128]{3,2,1,0:T(8,128)(2,1)} collective-permute-done((bf16[2,16,128,128]{3,2,1,0:T(8,128)(2,1)}, bf16[2,16,128,128]{3,2,1,0:T(8,128)(2,1)}, u32[]{:S(2)}, u32[]{:S(2)}) %collective-permute-start) | collective-permute-done | bytes 1048608 | tf_op jit(solution)/shard_map/while/body/eval_jaxpr/ppermute | solution.py:18
  1118.8 21.5 %collective-permute-done = bf16[2,16,128,128]{3,2,1,0:T(8,128)(2,1)} collective-permute-done((bf16[2,16,128,128]{3,2,1,0:T(8,128)(2,1)}, bf16[2,16,128,128]{3,2,1,0:T(8,128)(2,1)}, u32[]{:S(2)}, u32[]{:S(2)}) %collective-permute-start) | collective-permute-done | bytes 1048608 | tf_op jit(solution)/shard_map/while/body/eval_jaxpr/ppermute | solution.py:18
  1149.4 47.7 %while.78 = (s32[]{:T(128)}, f32[16,128,128]{2,1,0:T(8,128)S(1)}, f32[4,16,64,128]{3,2,1,0:T(8,128)}, s32[4]{0:T(128)S(1)}, s32[]{:T(128)}, /*index=5*/f32[4,16,...) while((s32[]{:T(128)}, f32[16,128,128]{2,1,0:T(8,128)S(1)}, ...), condition=%wide.region_8.10_spmd.clone, body=%wide.region_7.9_spmd.clone.sunk | while | flops 806690816 | bytes 19451036 | solution.py:102
  1209.4 11.7 collective-permute-done.2
  1222.6 12.3 fusion.115
  1244.9 5.2 broadcast_multiply_fusion
  1255.6 316.2 %custom-call.7 = f32[4,16,1,64,64]{3,4,2,1,0:T(8,128)} custom-call(f32[4,16,1,64,64]{4,3,2,1,0:T(8,128)} %add_bitcast_fusion), custom_call_target="InvertDiagBlocksLowerTriangular" | custom-call | tf_op jit(solution)/shard_map/triangular_solve/custom-call.1 | solution.py:44
  1571.8 6.6 fusion.111
  1581.0 54.3 %while.81 = (s32[]{:T(128)}, f32[16,128,128]{2,1,0:T(8,128)S(1)}, f32[16,128,128]{2,1,0:T(8,128)}, s32[4]{0:T(128)S(1)}, s32[]{:T(128)}, /*index=5*/f32[4,16,64,...) while((s32[]{:T(128)}, f32[16,128,128]{2,1,0:T(8,128)S(1)}, ...), condition=%wide.region_13.15_spmd.clone, body=%wide.region_12.14_spmd.clone.sunk | while | flops 807534592 | bytes 19401408 | solution.py:135
  1639.0 233.4 %while.77 = (s32[]{:T(128)}, f32[2,16,128,128]{3,2,1,0:T(8,128)}, pred[]{:T(512)}, f32[16,128,128]{2,1,0:T(8,128)S(1)}, f32[16,128,128]{2,1,0:T(8,128)}, /*index=5*/f32[2,16,128,128]{3,2,1,0:T(8,128)S(1)}, s32[]{:T(128)}) while((s32[]{:T(128)}, f32[2,16,128,128]{3,2,1,0:T(8,128)}, pred[]{:T(512)}, f32[16,128,128]{2,1,0:T(8,128)S(1)}, ...), condition=%wide.region_15.17_spmd, body=%wide.region_14.16_spmd.sunk | while | flops 807665664 | bytes 22020240 | solution.py:189
  1646.5 25.9 %collective-permute-done.1 = bf16[2,16,128,128]{3,2,1,0:T(8,128)(2,1)} collective-permute-done((bf16[2,16,128,128]{3,2,1,0:T(8,128)(2,1)}, bf16[2,16,128,128]{3,2,1,0:T(8,128)(2,1)}, u32[]{:S(2)}, u32[]{:S(2)}) %collective-permute-start.1) | collective-permute-done | bytes 1048608 | tf_op jit(solution)/shard_map/while/body/eval_jaxpr/ppermute | solution.py:18
  1682.5 25.1 %collective-permute-done.1 = bf16[2,16,128,128]{3,2,1,0:T(8,128)(2,1)} collective-permute-done((bf16[2,16,128,128]{3,2,1,0:T(8,128)(2,1)}, bf16[2,16,128,128]{3,2,1,0:T(8,128)(2,1)}, u32[]{:S(2)}, u32[]{:S(2)}) %collective-permute-start.1) | collective-permute-done | bytes 1048608 | tf_op jit(solution)/shard_map/while/body/eval_jaxpr/ppermute | solution.py:18
  1717.7 24.1 %collective-permute-done.1 = bf16[2,16,128,128]{3,2,1,0:T(8,128)(2,1)} collective-permute-done((bf16[2,16,128,128]{3,2,1,0:T(8,128)(2,1)}, bf16[2,16,128,128]{3,2,1,0:T(8,128)(2,1)}, u32[]{:S(2)}, u32[]{:S(2)}) %collective-permute-start.1) | collective-permute-done | bytes 1048608 | tf_op jit(solution)/shard_map/while/body/eval_jaxpr/ppermute | solution.py:18
  1752.0 23.2 %collective-permute-done.1 = bf16[2,16,128,128]{3,2,1,0:T(8,128)(2,1)} collective-permute-done((bf16[2,16,128,128]{3,2,1,0:T(8,128)(2,1)}, bf16[2,16,128,128]{3,2,1,0:T(8,128)(2,1)}, u32[]{:S(2)}, u32[]{:S(2)}) %collective-permute-start.1) | collective-permute-done | bytes 1048608 | tf_op jit(solution)/shard_map/while/body/eval_jaxpr/ppermute | solution.py:18
  1785.3 22.3 %collective-permute-done.1 = bf16[2,16,128,128]{3,2,1,0:T(8,128)(2,1)} collective-permute-done((bf16[2,16,128,128]{3,2,1,0:T(8,128)(2,1)}, bf16[2,16,128,128]{3,2,1,0:T(8,128)(2,1)}, u32[]{:S(2)}, u32[]{:S(2)}) %collective-permute-start.1) | collective-permute-done | bytes 1048608 | tf_op jit(solution)/shard_map/while/body/eval_jaxpr/ppermute | solution.py:18
  1817.7 21.4 %collective-permute-done.1 = bf16[2,16,128,128]{3,2,1,0:T(8,128)(2,1)} collective-permute-done((bf16[2,16,128,128]{3,2,1,0:T(8,128)(2,1)}, bf16[2,16,128,128]{3,2,1,0:T(8,128)(2,1)}, u32[]{:S(2)}, u32[]{:S(2)}) %collective-permute-start.1) | collective-permute-done | bytes 1048608 | tf_op jit(solution)/shard_map/while/body/eval_jaxpr/ppermute | solution.py:18
  1849.1 20.4 %collective-permute-done.1 = bf16[2,16,128,128]{3,2,1,0:T(8,128)(2,1)} collective-permute-done((bf16[2,16,128,128]{3,2,1,0:T(8,128)(2,1)}, bf16[2,16,128,128]{3,2,1,0:T(8,128)(2,1)}, u32[]{:S(2)}, u32[]{:S(2)}) %collective-permute-start.1) | collective-permute-done | bytes 1048608 | tf_op jit(solution)/shard_map/while/body/eval_jaxpr/ppermute | solution.py:18
  1876.6 44.2 %while.79 = (s32[]{:T(128)}, f32[16,128,128]{2,1,0:T(8,128)S(1)}, f32[4,16,64,128]{3,2,1,0:T(8,128)}, s32[4]{0:T(128)S(1)}, s32[]{:T(128)}, /*index=5*/f32[4,16,...) while((s32[]{:T(128)}, f32[16,128,128]{2,1,0:T(8,128)S(1)}, ...), condition=%wide.region_19.21_spmd.clone, body=%wide.region_18.20_spmd.clone.sunk | while | flops 806690816 | bytes 12109449 | solution.py:102
  (343 shorter events, 367.7 us)
Async XLA Ops:
  6.5 1136.8 %copy-start = (f32[1,16,128,128]{3,2,1,0:T(8,128)S(1)}, f32[1,16,128,128]{3,2,1,0:T(8,128)}, u32[]{:S(2)}) copy-start(f32[1,16,128,128]{3,2,1,0:T(8,128)} %param.28) | copy-start | bytes 3145732
  6.5 64.4 %copy-start.17 = (bf16[1,256,2048]{2,1,0:T(8,128)(2,1)S(1)}, bf16[1,256,2048]{2,1,0:T(8,128)(2,1)}, u32[]{:S(2)}) copy-start(bf16[1,256,2048]{2,1,0:T(8,128)(2,1)} %param.22) | copy-start | bytes 3145732
  6.5 64.7 %copy-start.22 = (f32[1,2048]{1,0:T(1,128)S(1)}, f32[1,2048]{1,0:T(1,128)}, u32[]{:S(2)}) copy-start(f32[1,2048]{1,0:T(1,128)} %param.26) | copy-start | bytes 24580
  6.5 64.7 %copy-start.23 = (f32[1,16]{1,0:T(1,128)S(1)}, f32[1,16]{1,0:T(1,128)}, u32[]{:S(2)}) copy-start(f32[1,16]{1,0:T(1,128)} %param.25) | copy-start | bytes 196
  6.5 483.5 %all-gather.4.cloned.1.call-start = ((), (), s32[]{:S(2)}) async-start(), calls=%async_computation.1 | async-start | bytes 28311552 | tf_op jit(solution)/shard_map/all_gather | solution.py:163
  7.3 1631.8 %all-reduce.3.cloned.1.call-start = ((), (), s32[]{:S(2)}) async-start(), calls=%async_computation | async-start | bytes 1048576 | tf_op jit(solution)/shard_map/psum | solution.py:23
  72.2 2.6 copy-start.21
  911.1 2.5 copy-start.9
  915.9 27.3 %collective-permute-start = (bf16[2,16,128,128]{3,2,1,0:T(8,128)(2,1)}, bf16[2,16,128,128]{3,2,1,0:T(8,128)(2,1)}, u32[]{:S(2)}, u32[]{:S(2)}) collective-permute-start(bf16[2,16,128,128]{3,2,1,0:T(8,128)(2,1)} %pad_maximum_fusion.4), channel_id=1, source_target_pairs={{0,1},{1,2},{2,3},{3,4},{4,5},{5,6},{6,7},{8,9},{9,10},{10,11},{11... | collective-permute-start | bytes 3145736 | tf_op jit(solution)/shard_map/while/body/eval_jaxpr/ppermute | solution.py:18
  946.2 2.5 copy-start.9
  951.0 27.3 %collective-permute-start = (bf16[2,16,128,128]{3,2,1,0:T(8,128)(2,1)}, bf16[2,16,128,128]{3,2,1,0:T(8,128)(2,1)}, u32[]{:S(2)}, u32[]{:S(2)}) collective-permute-start(bf16[2,16,128,128]{3,2,1,0:T(8,128)(2,1)} %pad_maximum_fusion.4), channel_id=1, source_target_pairs={{0,1},{1,2},{2,3},{3,4},{4,5},{5,6},{6,7},{8,9},{9,10},{10,11},{11... | collective-permute-start | bytes 3145736 | tf_op jit(solution)/shard_map/while/body/eval_jaxpr/ppermute | solution.py:18
  986.1 26.5 %collective-permute-start = (bf16[2,16,128,128]{3,2,1,0:T(8,128)(2,1)}, bf16[2,16,128,128]{3,2,1,0:T(8,128)(2,1)}, u32[]{:S(2)}, u32[]{:S(2)}) collective-permute-start(bf16[2,16,128,128]{3,2,1,0:T(8,128)(2,1)} %pad_maximum_fusion.4), channel_id=1, source_target_pairs={{0,1},{1,2},{2,3},{3,4},{4,5},{5,6},{6,7},{8,9},{9,10},{10,11},{11... | collective-permute-start | bytes 3145736 | tf_op jit(solution)/shard_map/while/body/eval_jaxpr/ppermute | solution.py:18
  1020.3 25.5 %collective-permute-start = (bf16[2,16,128,128]{3,2,1,0:T(8,128)(2,1)}, bf16[2,16,128,128]{3,2,1,0:T(8,128)(2,1)}, u32[]{:S(2)}, u32[]{:S(2)}) collective-permute-start(bf16[2,16,128,128]{3,2,1,0:T(8,128)(2,1)} %pad_maximum_fusion.4), channel_id=1, source_target_pairs={{0,1},{1,2},{2,3},{3,4},{4,5},{5,6},{6,7},{8,9},{9,10},{10,11},{11... | collective-permute-start | bytes 3145736 | tf_op jit(solution)/shard_map/while/body/eval_jaxpr/ppermute | solution.py:18
  1053.7 24.6 %collective-permute-start = (bf16[2,16,128,128]{3,2,1,0:T(8,128)(2,1)}, bf16[2,16,128,128]{3,2,1,0:T(8,128)(2,1)}, u32[]{:S(2)}, u32[]{:S(2)}) collective-permute-start(bf16[2,16,128,128]{3,2,1,0:T(8,128)(2,1)} %pad_maximum_fusion.4), channel_id=1, source_target_pairs={{0,1},{1,2},{2,3},{3,4},{4,5},{5,6},{6,7},{8,9},{9,10},{10,11},{11... | collective-permute-start | bytes 3145736 | tf_op jit(solution)/shard_map/while/body/eval_jaxpr/ppermute | solution.py:18
  1086.1 23.7 %collective-permute-start = (bf16[2,16,128,128]{3,2,1,0:T(8,128)(2,1)}, bf16[2,16,128,128]{3,2,1,0:T(8,128)(2,1)}, u32[]{:S(2)}, u32[]{:S(2)}) collective-permute-start(bf16[2,16,128,128]{3,2,1,0:T(8,128)(2,1)} %pad_maximum_fusion.4), channel_id=1, source_target_pairs={{0,1},{1,2},{2,3},{3,4},{4,5},{5,6},{6,7},{8,9},{9,10},{10,11},{11... | collective-permute-start | bytes 3145736 | tf_op jit(solution)/shard_map/while/body/eval_jaxpr/ppermute | solution.py:18
  1117.6 22.8 %collective-permute-start = (bf16[2,16,128,128]{3,2,1,0:T(8,128)(2,1)}, bf16[2,16,128,128]{3,2,1,0:T(8,128)(2,1)}, u32[]{:S(2)}, u32[]{:S(2)}) collective-permute-start(bf16[2,16,128,128]{3,2,1,0:T(8,128)(2,1)} %pad_maximum_fusion.4), channel_id=1, source_target_pairs={{0,1},{1,2},{2,3},{3,4},{4,5},{5,6},{6,7},{8,9},{9,10},{10,11},{11... | collective-permute-start | bytes 3145736 | tf_op jit(solution)/shard_map/while/body/eval_jaxpr/ppermute | solution.py:18
  1143.3 2.9 copy-start.16
  1197.1 5.5 copy-start.4
  1203.9 2.7 copy-start.3
  1206.5 14.5 collective-permute-start.2
  1596.2 2.7 copy-start.6
  1609.9 2.7 copy-start.6
  1623.6 2.7 copy-start.6
  1645.2 27.2 %collective-permute-start.1 = (bf16[2,16,128,128]{3,2,1,0:T(8,128)(2,1)}, bf16[2,16,128,128]{3,2,1,0:T(8,128)(2,1)}, u32[]{:S(2)}, u32[]{:S(2)}) collective-permute-start(bf16[2,16,128,128]{3,2,1,0:T(8,128)(2,1)} %pad_maximum_fusion.5), channel_id=1, source_target_pairs={{0,1},{1,2},{2,3},{3,4},{4,5},{5,6},{6,7},{8,9},{9,10},{10,11},{11... | collective-permute-start | bytes 3145736 | tf_op jit(solution)/shard_map/while/body/eval_jaxpr/ppermute | solution.py:18
  1681.3 26.4 %collective-permute-start.1 = (bf16[2,16,128,128]{3,2,1,0:T(8,128)(2,1)}, bf16[2,16,128,128]{3,2,1,0:T(8,128)(2,1)}, u32[]{:S(2)}, u32[]{:S(2)}) collective-permute-start(bf16[2,16,128,128]{3,2,1,0:T(8,128)(2,1)} %pad_maximum_fusion.5), channel_id=1, source_target_pairs={{0,1},{1,2},{2,3},{3,4},{4,5},{5,6},{6,7},{8,9},{9,10},{10,11},{11... | collective-permute-start | bytes 3145736 | tf_op jit(solution)/shard_map/while/body/eval_jaxpr/ppermute | solution.py:18
  1716.4 25.4 %collective-permute-start.1 = (bf16[2,16,128,128]{3,2,1,0:T(8,128)(2,1)}, bf16[2,16,128,128]{3,2,1,0:T(8,128)(2,1)}, u32[]{:S(2)}, u32[]{:S(2)}) collective-permute-start(bf16[2,16,128,128]{3,2,1,0:T(8,128)(2,1)} %pad_maximum_fusion.5), channel_id=1, source_target_pairs={{0,1},{1,2},{2,3},{3,4},{4,5},{5,6},{6,7},{8,9},{9,10},{10,11},{11... | collective-permute-start | bytes 3145736 | tf_op jit(solution)/shard_map/while/body/eval_jaxpr/ppermute | solution.py:18
  1750.7 24.5 %collective-permute-start.1 = (bf16[2,16,128,128]{3,2,1,0:T(8,128)(2,1)}, bf16[2,16,128,128]{3,2,1,0:T(8,128)(2,1)}, u32[]{:S(2)}, u32[]{:S(2)}) collective-permute-start(bf16[2,16,128,128]{3,2,1,0:T(8,128)(2,1)} %pad_maximum_fusion.5), channel_id=1, source_target_pairs={{0,1},{1,2},{2,3},{3,4},{4,5},{5,6},{6,7},{8,9},{9,10},{10,11},{11... | collective-permute-start | bytes 3145736 | tf_op jit(solution)/shard_map/while/body/eval_jaxpr/ppermute | solution.py:18
  1784.0 23.6 %collective-permute-start.1 = (bf16[2,16,128,128]{3,2,1,0:T(8,128)(2,1)}, bf16[2,16,128,128]{3,2,1,0:T(8,128)(2,1)}, u32[]{:S(2)}, u32[]{:S(2)}) collective-permute-start(bf16[2,16,128,128]{3,2,1,0:T(8,128)(2,1)} %pad_maximum_fusion.5), channel_id=1, source_target_pairs={{0,1},{1,2},{2,3},{3,4},{4,5},{5,6},{6,7},{8,9},{9,10},{10,11},{11... | collective-permute-start | bytes 3145736 | tf_op jit(solution)/shard_map/while/body/eval_jaxpr/ppermute | solution.py:18
  1816.4 22.7 %collective-permute-start.1 = (bf16[2,16,128,128]{3,2,1,0:T(8,128)(2,1)}, bf16[2,16,128,128]{3,2,1,0:T(8,128)(2,1)}, u32[]{:S(2)}, u32[]{:S(2)}) collective-permute-start(bf16[2,16,128,128]{3,2,1,0:T(8,128)(2,1)} %pad_maximum_fusion.5), channel_id=1, source_target_pairs={{0,1},{1,2},{2,3},{3,4},{4,5},{5,6},{6,7},{8,9},{9,10},{10,11},{11... | collective-permute-start | bytes 3145736 | tf_op jit(solution)/shard_map/while/body/eval_jaxpr/ppermute | solution.py:18
  1847.9 21.7 %collective-permute-start.1 = (bf16[2,16,128,128]{3,2,1,0:T(8,128)(2,1)}, bf16[2,16,128,128]{3,2,1,0:T(8,128)(2,1)}, u32[]{:S(2)}, u32[]{:S(2)}) collective-permute-start(bf16[2,16,128,128]{3,2,1,0:T(8,128)(2,1)} %pad_maximum_fusion.5), channel_id=1, source_target_pairs={{0,1},{1,2},{2,3},{3,4},{4,5},{5,6},{6,7},{8,9},{9,10},{10,11},{11... | collective-permute-start | bytes 3145736 | tf_op jit(solution)/shard_map/while/body/eval_jaxpr/ppermute | solution.py:18
  1872.4 4.1 copy-start.10
  1925.0 3.9 copy-start.1
  (33 other events, 70.2 us)
Sparse Core Ops, SparseCore 0:
  8.9 481.0 all-gather.3
  1209.5 73.7 all-reduce.2
where the time goes:
time: 1950 us; the launch traced here: 1940 us
  waiting for transfers between devices  759 us (39%)
  other arithmetic  725 us (37%)
  matrix products  257 us (13%)
  local copies, waits for them, and re-layouts  77.1 us (4%)
  blocking collectives  63.6 us (3%)
  loops' own time  22.2 us (1%)
    another operation x5, other arithmetic, block_solve(): lax.linalg.triangular_solve(system, right_side, left_side=True, lower=Tru...  632 us
    all_gather x1, waiting for transfers between devices, shards(): lax.all_gather(w_qkv[0], 'seq', axis=0, tiled=True)  415 us
    ppermute x14, waiting for transfers between devices, from_behind(): return lax.ppermute(value, axis, pairs)  331 us
    all_gather x1, blocking collectives, shards(): lax.all_gather(w_beta[0], 'seq', axis=0, tiled=True)  63.6 us
    select_n x14, other arithmetic, hop_once(): return jnp.where(position == 0, empty_map, passed)  40.9 us
  transfers between devices with their start and end apart: 17, of which 16 were waited for; matrix products, arithmetic and copies ran while one was open for 21% of the time, Pallas kernels for 0%

commit v1 on v0

v1 whole, which is shorter than its diff:
```python
import functools

import jax
import jax.numpy as jnp
from jax import lax
from jax.experimental import pallas as pl
from jax.experimental.pallas import tpu as pltpu
from jax.sharding import PartitionSpec as P

HEADS = 16
HD = 128
GROUP = 64
TICKS = 2
CHUNK = 128
F32 = jnp.float32
BF16 = jnp.bfloat16


def mm(a, b):
    return jnp.dot(a.astype(BF16), b.astype(BF16), preferred_element_type=F32)


def mm_nt(a, b):
    return lax.dot_general(
        a.astype(BF16), b.astype(BF16), (((1,), (1,)), ((), ())), preferred_element_type=F32
    )


def unit_norm(p):
    return p * lax.rsqrt(jnp.sum(p * p, axis=-1, keepdims=True) + 1e-06)


def layer_rows(normed, w, bias, out_gain, residual, state, heads, doc_block, first_block):
    rows = normed.shape[0]
    width = heads * HD
    projected = jnp.dot(normed, w, preferred_element_type=F32)
    row = lax.broadcasted_iota(jnp.int32, (CHUNK, CHUNK), 0)
    col = lax.broadcasted_iota(jnp.int32, (CHUNK, CHUNK), 1)
    row1 = lax.broadcasted_iota(jnp.int32, (CHUNK, 1), 0)
    eye = (row == col).astype(F32)
    problems = []
    for h in range(heads):
        q_all = unit_norm(projected[:, h * HD : (h + 1) * HD]).astype(BF16)
        k_all = unit_norm(projected[:, width + h * HD : width + (h + 1) * HD])
        k_all = k_all.astype(BF16).astype(F32)
        v_all = projected[:, 2 * width + h * HD : 2 * width + (h + 1) * HD]
        beta_all = jax.nn.sigmoid(
            projected[:, 3 * width + h : 3 * width + h + 1] + bias[:, h : h + 1]
        )
        for c in range(rows // CHUNK):
            at = slice(c * CHUNK, (c + 1) * CHUNK)
            problems.append((h, c, q_all[at], k_all[at], v_all[at], beta_all[at]))
    systems, inverses, masks = [], [], []
    for h, c, q, k, v, beta in problems:
        start = (doc_block - first_block) * GROUP - c * CHUNK
        inside = jnp.logical_and(start >= 0, start < CHUNK)
        cut = jnp.where(inside, start, 0)
        late_row = row >= cut
        late_col = col >= cut
        same = late_row == late_col
        from_entry = jnp.where(inside, (row1 < cut).astype(F32), 1.0)
        to_exit = (row1 >= cut).astype(F32)
        keep = jnp.where(inside, 0.0, 1.0)
        system = jnp.where(jnp.logical_and(row > col, same), mm_nt(k * beta, k), 0.0)
        systems.append(system)
        masks.append((same, from_entry, to_exit, keep))
        inverses.append(eye - jnp.where((row // 2) == (col // 2), system, 0.0))
    size = 2
    while size < CHUNK:
        level = jnp.logical_and(
            (row // (2 * size)) == (col // (2 * size)), (row // size) != (col // size)
        )
        halves = [mm(jnp.where(level, s, 0.0), x) for s, x in zip(systems, inverses)]
        inverses = [x - mm(x, b) for x, b in zip(inverses, halves)]
        size *= 2
    steps = {}
    for (h, c, q, k, v, beta), inverse, (same, from_entry, to_exit, keep) in zip(
        problems, inverses, masks
    ):
        solved = mm(inverse, jnp.concatenate([v * beta, k * (beta * from_entry)], axis=1))
        scores = jnp.where(jnp.logical_and(row >= col, same), mm_nt(q, k), 0.0)
        lhs = jnp.concatenate([scores, jnp.transpose(k * to_exit)], axis=0)
        both = mm(lhs, solved)
        add = both[:, :HD]
        q_in = q.astype(F32) * from_entry
        through = jnp.concatenate([q_in - both[:CHUNK, HD:], -both[CHUNK:, HD:]], axis=0)
        steps[h, c] = (through.astype(BF16), add, keep)
    pieces = []
    for c in range(rows // CHUNK):
        for h in range(heads):
            through, add, keep = steps[h, c]
            now = state[h]
            moved = jnp.dot(through, now.astype(BF16), preferred_element_type=F32) + add
            state[h] = now * keep + moved[CHUNK:]
            pieces.append(moved[:CHUNK])
    columns = []
    for h in range(heads):
        o = jnp.concatenate([pieces[c * heads + h] for c in range(rows // CHUNK)], axis=0)
        columns.append(
            o * lax.rsqrt(jnp.mean(o * o, axis=-1, keepdims=True) + 1e-05) * out_gain
        )
    mixed = jnp.concatenate(columns, axis=1) if heads > 1 else columns[0]
    return (residual.astype(F32) + mixed).astype(BF16)


def layer_kernel(heads, parts, info, x, w, bias, in_gain, out_gain, entry, out, final):
    step = pl.program_id(0)
    width = heads * HD

    @pl.when(step == 0)
    def _():
        final[...] = entry[...]

    if parts:
        wide = jnp.concatenate([x[c] for c in range(parts)], axis=1).astype(F32)
        residual = x[info[1]]
    else:
        wide = x[...].astype(F32)
        residual = x[:, pl.ds(pl.multiple_of(info[1] * width, HD), width)]
    normed = wide * lax.rsqrt(jnp.mean(wide * wide, axis=-1, keepdims=True) + 1e-05) * in_gain[...]
    rows = wide.shape[0]
    state = [final[h] for h in range(heads)]
    out[...] = layer_rows(
        normed.astype(BF16), w[...], bias[...], out_gain[...], residual, state, heads,
        info[0], step * (rows // GROUP),
    )
    for h in range(heads):
        final[h] = state[h]


def layer(x, w, bias, in_gain, out_gain, entry, info, heads, rows=512):
    parts = x.shape[0] if x.ndim == 3 else 0
    total, d = x.shape[-2], in_gain.shape[-1]
    width = heads * HD
    if parts:
        x_spec = pl.BlockSpec((parts, rows, x.shape[2]), lambda i, s: (0, i, 0))
    else:
        x_spec = pl.BlockSpec((rows, d), lambda i, s: (i, 0))

    def whole(shape):
        return pl.BlockSpec(shape, lambda i, s: (0,) * len(shape))

    return pl.pallas_call(
        functools.partial(layer_kernel, heads, parts),
        out_shape=(
            jax.ShapeDtypeStruct((total, width), BF16),
            jax.ShapeDtypeStruct((heads, HD, HD), F32),
        ),
        grid_spec=pltpu.PrefetchScalarGridSpec(
            num_scalar_prefetch=1,
            grid=(total // rows,),
            in_specs=[
                x_spec,
                whole(w.shape),
                whole(bias.shape),
                whole(in_gain.shape),
                whole(out_gain.shape),
                whole(entry.shape),
            ],
            out_specs=(
                pl.BlockSpec((rows, width), lambda i, s: (i, 0)),
                whole((heads, HD, HD)),
            ),
        ),
        compiler_params=pltpu.CompilerParams(vmem_limit_bytes=50 * 2**20),
        name="layer",
    )(info, x, w, bias, in_gain, out_gain, entry)


def shards(residual, w_qkv, w_beta, beta_bias, norm_gain, out_gain, state_in, doc_start):
    count = lax.axis_size("seq")
    place = lax.axis_index("seq")
    heads = HEADS // count
    width = heads * HD
    depth = w_qkv.shape[1]
    weights = jnp.concatenate(
        [
            w_qkv[0].reshape(depth, 3, count, width).transpose(2, 0, 1, 3).reshape(count, depth, 3 * width),
            jnp.pad(
                w_beta[0].reshape(depth, count, heads).transpose(1, 0, 2),
                ((0, 0), (0, 0), (0, HD - heads)),
            ),
        ],
        axis=2,
    )
    weights = lax.all_to_all(weights, "seq", 0, 0, tiled=True).reshape(count * depth, 3 * width + HD)
    stream = lax.all_gather(residual[0], "seq", axis=0, tiled=True)
    bias = lax.dynamic_slice(beta_bias, (0, place * heads), (1, heads))
    bias = jnp.pad(bias, ((0, 0), (0, HD - heads)))
    state = lax.dynamic_slice(state_in[0], (place * heads, 0, 0), (heads, HD, HD))
    out = None
    for tick in range(TICKS):
        if tick:
            out = lax.ppermute(
                out, "section", [(i, (i + 1) % lax.axis_size("section")) for i in range(lax.axis_size("section"))]
            )
            stream = lax.all_gather(out, "seq", axis=0)
        info = jnp.stack([doc_start[tick, 0], place]).astype(jnp.int32)
        out, state = layer(stream, weights, bias, norm_gain, out_gain, state, info, heads)
    back = lax.all_to_all(out.reshape(count, -1, width), "seq", 0, 0, tiled=True)
    return back.transpose(1, 0, 2).reshape(1, -1, count * width)


def solution(mesh):
    return jax.shard_map(
        shards,
        mesh=mesh,
        in_specs=(
            P("section", "seq", None),
            P("section", "seq", None),
            P("section", "seq", None),
            P("section", None),
            P("section", None),
            P("section", None),
            P("section", None, None, None),
            P(None, "section"),
        ),
        out_specs=P("section", "seq", None),
        check_vma=False,
    )
```

time: 1950 us -> 440 us (0.23)
  other arithmetic: 725 us -> 5.44 us
  waiting for transfers between devices: 759 us -> 305 us
  matrix products: 257 us -> 0 us
  local copies, waits for them, and re-layouts: 77.1 us -> 18.5 us
  Pallas kernels: 0 us -> 57 us
  blocking collectives: 63.6 us -> 29.5 us
  loops' own time: 22.2 us -> 0 us
    another operation x19 -> x2, other arithmetic: 647 us -> 1.47 us  [shards(): info = jnp.stack([doc_start[tick, 0], place]).astype(jnp.int32)]
    ppermute x15 -> x1, waiting for transfers between devices: 343 us -> 14.2 us  [shards(): lax.ppermute(out, 'section', [(i, (i + 1) % lax.axis_size('section')) for...]
    all_gather x1 -> x2, waiting for transfers between devices: 415 us -> 137 us  [the longest x1 122 us: shards(): stream = lax.all_gather(out, 'seq', axis=0)]
    dot_general x108 -> x0, matrix products: 244 us -> none  [the longest x14 34.7 us: compose(): jnp.einsum('hij,hjk->hik', latter[0], earlier[0], precision=FULL_PRECISION)]
    all_to_all x0 -> x1, waiting for transfers between devices: none -> 153 us  [shards(): lax.all_to_all(weights, 'seq', 0, 0, tiled=True)]
    all_gather x1 -> x0, blocking collectives: 63.6 us -> none  [shards(): lax.all_gather(w_beta[0], 'seq', axis=0, tiled=True)]
    pallas_call x0 -> x2, Pallas kernels: none -> 57 us  [layer(): pl.pallas_call(functools.partial(layer_kernel, heads, parts), out_shape=(...]
    select_n x23 -> x0, other arithmetic: 41.8 us -> none  [the longest x14 40.9 us: hop_once(): return jnp.where(position == 0, empty_map, passed)]
  transfers between devices with their start and end apart: 17 -> 4, of which waited for: 16 -> 4; matrix products, arithmetic and copies ran while one was open for 21% -> 5% of each run, Pallas kernels for 0% -> 0%
where the time goes in v1:
time: 440 us; the launch traced here: 435 us
  waiting for transfers between devices  305 us (69%)
  Pallas kernels  57 us (13%)
  blocking collectives  29.5 us (7%)
  local copies, waits for them, and re-layouts  18.5 us (4%)
  between operations  13.4 us (3%)
  starting transfers between devices  6.42 us (1%)
  other arithmetic  5.44 us (1%)
    all_to_all x1, waiting for transfers between devices, shards(): lax.all_to_all(weights, 'seq', 0, 0, tiled=True)  153 us
    all_gather x1, waiting for transfers between devices, shards(): stream = lax.all_gather(out, 'seq', axis=0)  122 us
    pallas_call x2, Pallas kernels, layer(): pl.pallas_call(functools.partial(layer_kernel, heads, parts), out_shape=(...  57 us
    all_to_all x1, blocking collectives, shards(): lax.all_to_all(out.reshape(count, -1, width), 'seq', 0, 0, tiled=True)  29.5 us
    all_gather x1, waiting for transfers between devices, shards(): stream = lax.all_gather(residual[0], 'seq', axis=0, tiled=True)  14.7 us
    ppermute x1, waiting for transfers between devices, shards(): lax.ppermute(out, 'section', [(i, (i + 1) % lax.axis_size('section')) for...  14.2 us
  transfers between devices with their start and end apart: 4, of which 4 were waited for; matrix products, arithmetic and copies ran while one was open for 5% of the time, Pallas kernels for 0%

profile of v1, /device:TPU:28, one launch (start us, length us, event | category | flops | bytes accessed | tf_op | source)
XLA Modules:
  0.0 435.3 jit_solution(1866569736822303536)
XLA Ops:
  6.5 0.0 copy-start
  6.5 0.0 all-gather.5.cloned.1.call-start
  6.5 0.7 all-gather.5.cloned.1.call-update
  7.3 4.7 %copy.14 = bf16[1,256,6144]{1,2,0:T(8,128)(2,1)} copy(bf16[1,256,6144]{2,1,0:T(8,128)(2,1)} %param.9) | data formatting | bytes 6291456 | tf_op args[1]
  12.0 3.9 copy.15
  15.9 0.0 copy-done.4
  15.9 4.0 fusion.1
  19.9 6.1 %all-to-all-start = ((bf16[8,256,896]{1,2,0:T(8,128)(2,1)}), bf16[8,256,896]{1,2,0:T(8,128)(2,1)}, u32[]{:S(2)}, u32[]{:S(2)}) async-start(bf16[8,256,896]{1,2,0:T(8,128)(2,1)} %fusion.1), calls=%async_computation | async-start | bytes 7340032 | tf_op jit(solution)/shard_map/all_to_all | solution.py:186
  26.0 0.0 all-gather.7.cloned.1.call-start
  26.0 0.0 copy-done.6
  26.0 0.1 constant_dynamic-slice_fusion
  26.1 0.0 copy-done.5
  26.1 0.6 fusion.2
  26.8 0.7 pad_add_fusion.1.info
  27.5 0.0 copy-done
  27.5 0.0 copy-start.1
  27.5 0.0 copy-start.2
  27.5 153.1 %all-to-all-done = bf16[8,256,896]{1,2,0:T(8,128)(2,1)} async-done(((bf16[8,256,896]{1,2,0:T(8,128)(2,1)}), bf16[8,256,896]{1,2,0:T(8,128)(2,1)}, u32[]{:S(2)}, u32[]{:S(2)}) %all-to-all-start) | async-done | bytes 3670048 | tf_op jit(solution)/shard_map/all_to_all | solution.py:186
  180.6 6.2 %copy.16 = bf16[8,256,896]{2,1,0:T(8,128)(2,1)} copy(bf16[8,256,896]{1,2,0:T(8,128)(2,1)} %all-to-all-done) | data formatting | bytes 7340032 | tf_op jit(solution)/shard_map/all_to_all | solution.py:186
  186.9 14.7 %all-gather.5.cloned.1.call-done = bf16[1,2048,2048]{2,1,0:T(8,128)(2,1)} async-done(((bf16[1,256,2048]{2,1,0:T(8,128)(2,1)}), bf16[1,2048,2048]{2,1,0:T(8,128)(2,1)}) %all-gather.5.cloned.1.call-update) | async-done | bytes 8388624 | tf_op jit(solution)/shard_map/all_gather | solution.py:187
  201.5 0.0 copy-done.1
  201.5 28.7 %layer.2 = (bf16[2048,256]{1,0:T(8,128)(2,1)S(1)}, f32[2,128,128]{2,1,0:T(8,128)S(1)}) custom-call(s32[2]{0:T(128)S(1)} %pad_add_fusion.1.info, bf16[2048,2048]{1,0:T(8,128)(2,1)} %bitcast.22, bf16[2048,896]{1,0:T(8,128)(2,1)} %bitcast.18, f32[1,128]{1,0:T(1,128)S(1)} %pad.9.bias, f32[1,2048]{1,0:T(1,128)S(1)} %copy-done.1, f32[1,128]{1,0:T(1,128)S(1)} %copy-done.2, ...), custom_call_target="tpu_custom_call" | custom-call | tf_op jit(solution)/shard_map/layer/pallas_call | solution.py:143
  230.2 0.3 collective-permute-start
  230.5 14.2 %collective-permute-done = bf16[2048,256]{1,0:T(8,128)(2,1)S(1)} collective-permute-done((bf16[2048,256]{1,0:T(8,128)(2,1)S(1)}, bf16[2048,256]{1,0:T(8,128)(2,1)S(1)}, u32[]{:S(2)}, u32[]{:S(2)}) %collective-permute-start) | collective-permute-done | bytes 1048608 | tf_op jit(solution)/shard_map/ppermute | solution.py:194
  244.7 1.0 copy-done.3
  245.7 0.0 all-gather.7.cloned.1.call-update
  245.7 0.7 pad_add_fusion.info
  246.4 122.3 %all-gather.7.cloned.1.call-done = bf16[16384,256]{1,0:T(8,128)(2,1)} async-done(((bf16[2048,256]{1,0:T(8,128)(2,1)}), bf16[16384,256]{1,0:T(8,128)(2,1)}) %all-gather.7.cloned.1.call-update) | async-done | bytes 8388624 | tf_op jit(solution)/shard_map/all_gather | solution.py:197
  368.7 28.4 %layer.3 = (bf16[2048,256]{1,0:T(8,128)(2,1)S(1)}, f32[2,128,128]{2,1,0:T(8,128)}) custom-call(s32[2]{0:T(128)S(1)} %pad_add_fusion.info, bf16[8,2048,256]{2,1,0:T(8,128)(2,1)} %bitcast.23, bf16[2048,896]{1,0:T(8,128)(2,1)} %bitcast.19, f32[1,128]{1,0:T(1,128)S(1)} %pad.9.bias, f32[1,2048]{1,0:T(1,128)S(1)} %copy-done.1, f32[1,128]{1,0:T(1,128)S(1)} %copy-done.2, ...), custom_call_target="tpu_custom_call" | custom-call | tf_op jit(solution)/shard_map/layer/pallas_call | solution.py:143
  397.1 29.5 %all_to_all.10 = bf16[8,256,256]{2,1,0:T(8,128)(2,1)S(1)} all-to-all(bf16[8,256,256]{2,1,0:T(8,128)(2,1)S(1)} %bitcast.17), channel_id=1, replica_groups=mesh['section'=4,'seq'=8] {'seq'}, dimensions={0} | all-to-all | bytes 2097152 | tf_op jit(solution)/shard_map/all_to_all | solution.py:200
  426.6 0.6 copy.17
  427.2 1.3 reshape.16
  (8 shorter events, 0.0 us)
Async XLA Ops:
  6.5 20.9 %copy-start = (f32[1,16,128,128]{3,2,1,0:T(8,128)S(1)}, f32[1,16,128,128]{3,2,1,0:T(8,128)}, u32[]{:S(2)}) copy-start(f32[1,16,128,128]{3,2,1,0:T(8,128)} %param.14) | copy-start | bytes 3145732
  6.5 195.0 %all-gather.5.cloned.1.call-start = ((), (), s32[]{:S(2)}) async-start(), calls=%async_computation.2 | async-start | bytes 9437184 | tf_op jit(solution)/shard_map/all_gather | solution.py:187
  12.0 3.9 copy-start.4
  19.9 6.1 %copy-start.6 = (f32[1,16]{1,0:T(1,128)S(1)}, f32[1,16]{1,0:T(1,128)}, u32[]{:S(2)}) copy-start(f32[1,16]{1,0:T(1,128)} %param.11) | copy-start | bytes 196
  19.9 6.2 %copy-start.5 = (s32[2,1]{0,1:T(1,128)S(1)}, s32[2,1]{0,1:T(1,128)}, u32[]{:S(2)}) copy-start(s32[2,1]{0,1:T(1,128)} %param.15) | copy-start | bytes 28
  19.9 160.8 %all-to-all-start = ((bf16[8,256,896]{1,2,0:T(8,128)(2,1)}), bf16[8,256,896]{1,2,0:T(8,128)(2,1)}, u32[]{:S(2)}, u32[]{:S(2)}) async-start(bf16[8,256,896]{1,2,0:T(8,128)(2,1)} %fusion.1), calls=%async_computation | async-start | bytes 7340032 | tf_op jit(solution)/shard_map/all_to_all | solution.py:186
  26.0 342.7 %all-gather.7.cloned.1.call-start = ((), (), s32[]{:S(2)}) async-start(), calls=%async_computation.3 | async-start | bytes 9437184 | tf_op jit(solution)/shard_map/all_gather | solution.py:197
  27.5 174.1 %copy-start.1 = (f32[1,2048]{1,0:T(1,128)S(1)}, f32[1,2048]{1,0:T(1,128)}, u32[]{:S(2)}) copy-start(f32[1,2048]{1,0:T(1,128)} %in_gain.3) | copy-start | bytes 24580
  27.5 174.0 %copy-start.2 = (f32[1,128]{1,0:T(1,128)S(1)}, f32[1,128]{1,0:T(1,128)}, u32[]{:S(2)}) copy-start(f32[1,128]{1,0:T(1,128)} %out_gain.3) | copy-start | bytes 1540
  230.2 14.5 %collective-permute-start = (bf16[2048,256]{1,0:T(8,128)(2,1)S(1)}, bf16[2048,256]{1,0:T(8,128)(2,1)S(1)}, u32[]{:S(2)}, u32[]{:S(2)}) collective-permute-start(bf16[2048,256]{1,0:T(8,128)(2,1)S(1)} %get-tuple-element.8), channel_id=1, source_target_pairs={{0,8},{8,16},{16,24},{24,0},{1,9},{9,17},{17,25},{25,1},{2,10},{10... | collective-permute-start | bytes 3145736 | tf_op jit(solution)/shard_map/ppermute | solution.py:194
  244.7 1.0 copy-start.3
Sparse Core Ops, SparseCore 0:
  9.5 192.0 all-gather.4
  245.8 122.8 all-gather.6

commit v2 on v1

--- a/solution.py
+++ b/solution.py
@@ -30,10 +30,13 @@
     return p * lax.rsqrt(jnp.sum(p * p, axis=-1, keepdims=True) + 1e-06)
 
 
-def layer_rows(normed, w, bias, out_gain, residual, state, heads, doc_block, first_block):
+def layer_rows(
+    normed, w, wb, bias, out_gain, residual, state, heads, first_head, doc_block, first_block
+):
     rows = normed.shape[0]
     width = heads * HD
     projected = jnp.dot(normed, w, preferred_element_type=F32)
+    logits = mm_nt(normed, wb) + bias
     row = lax.broadcasted_iota(jnp.int32, (CHUNK, CHUNK), 0)
     col = lax.broadcasted_iota(jnp.int32, (CHUNK, CHUNK), 1)
     row1 = lax.broadcasted_iota(jnp.int32, (CHUNK, 1), 0)
@@ -44,8 +47,9 @@
         k_all = unit_norm(projected[:, width + h * HD : width + (h + 1) * HD])
         k_all = k_all.astype(BF16).astype(F32)
         v_all = projected[:, 2 * width + h * HD : 2 * width + (h + 1) * HD]
+        mine = lax.broadcasted_iota(jnp.int32, logits.shape, 1) == first_head + h
         beta_all = jax.nn.sigmoid(
-            projected[:, 3 * width + h : 3 * width + h + 1] + bias[:, h : h + 1]
+            jnp.sum(jnp.where(mine, logits, 0.0), axis=-1, keepdims=True)
         )
         for c in range(rows // CHUNK):
             at = slice(c * CHUNK, (c + 1) * CHUNK)
@@ -103,7 +107,7 @@
     return (residual.astype(F32) + mixed).astype(BF16)
 
 
-def layer_kernel(heads, parts, info, x, w, bias, in_gain, out_gain, entry, out, final):
+def layer_kernel(heads, parts, info, x, w, wb, bias, in_gain, out_gain, entry, out, final):
     step = pl.program_id(0)
     width = heads * HD
 
@@ -121,14 +125,15 @@
     rows = wide.shape[0]
     state = [final[h] for h in range(heads)]
     out[...] = layer_rows(
-        normed.astype(BF16), w[...], bias[...], out_gain[...], residual, state, heads,
-        info[0], step * (rows // GROUP),
+        normed.astype(BF16), w[...],
+        jnp.concatenate([wb[c] for c in range(wb.shape[0])], axis=1),
+        bias[...], out_gain[...], residual, state, heads, info[1] * heads, info[0], step * (rows // GROUP),
     )
     for h in range(heads):
         final[h] = state[h]
 
 
-def layer(x, w, bias, in_gain, out_gain, entry, info, heads, rows=512):
+def layer(x, w, wb, bias, in_gain, out_gain, entry, info, heads, rows=512):
     parts = x.shape[0] if x.ndim == 3 else 0
     total, d = x.shape[-2], in_gain.shape[-1]
     width = heads * HD
@@ -152,6 +157,7 @@
             in_specs=[
                 x_spec,
                 whole(w.shape),
+                whole(wb.shape),
                 whole(bias.shape),
                 whole(in_gain.shape),
                 whole(out_gain.shape),
@@ -164,41 +170,330 @@
         ),
         compiler_params=pltpu.CompilerParams(vmem_limit_bytes=50 * 2**20),
         name="layer",
-    )(info, x, w, bias, in_gain, out_gain, entry)
+    )(info, x, w, wb, bias, in_gain, out_gain, entry)
+
+
+MESH = pl.DeviceIdType.MESH
+Z_CHIPS = 4
+
+
+def remote(src, dst, send, recv, **to):
+    return pltpu.make_async_remote_copy(
+        src_ref=src, dst_ref=dst, send_sem=send, recv_sem=recv, device_id=to, device_id_type=MESH
+    )
+
+
+def grid_place():
+    count = lax.axis_size("seq")
+    nz = min(Z_CHIPS, count)
+    ny = count // nz
+    place = lax.axis_index("seq")
+    return count, nz, ny, place, place // ny, lax.rem(place, ny)
+
+
+class Spread:
+    def __init__(self, slot, blocks, send, recv):
+        self.slot, self.blocks, self.send, self.recv = slot, blocks, send, recv
+        self.count, self.nz, self.ny, self.place, self.z, self.y = grid_place()
+        self.ways = [
+            (self.z + 1 < self.nz, self.place + self.ny),
+            (self.z > 0, self.place - self.ny),
+            (self.y + 1 < self.ny, self.place + 1),
+            (self.y > 0, self.place - 1),
+        ]
+
+    def neighbours(self):
+        return self.ways[: 4 if self.ny > 1 else 2]
+
+    def copy(self, way, source, block, ref=None):
+        here = self.slot(source, block)
+        return remote(
+            here if ref is None else ref,
+            here,
+            self.send.at[way, source, block],
+            self.recv.at[source, block],
+            seq=self.ways[way][1],
+        )
+
+    def go(self, way, source, block, ref=None):
+        if way >= 2 and self.ny == 1:
+            return
+
+        @pl.when(self.ways[way][0])
+        def _():
+            self.copy(way, source, block, ref).start()
+
+    def begin(self, block, ref=None):
+        for way in (0, 1, 2, 3):
+            self.go(way, self.place, block, ref)
+
+    def arrived(self, source, block):
+        self.copy(0, source, block).wait_recv()
+
+    def along_z(self, hop, block):
+        for way, sign in ((0, -1), (1, 1)):
+            z = self.z + sign * hop
+
+            @pl.when(jnp.logical_and(z >= 0, z < self.nz))
+            def _():
+                source = z * self.ny + self.y
+                self.arrived(source, block)
+                if hop + 1 < self.nz:
+                    self.go(way, source, block)
+                self.go(2, source, block)
+                self.go(3, source, block)
+
+    def along_y(self):
+        for hop in range(1, self.ny):
+            for way, sign in ((2, -1), (3, 1)):
+                y = self.y + sign * hop
+
+                @pl.when(jnp.logical_and(y >= 0, y < self.ny))
+                def _():
+                    def one(i, carry):
+                        source, block = (i // self.blocks) * self.ny + y, lax.rem(i, self.blocks)
+                        self.arrived(source, block)
+                        if hop + 1 < self.ny:
+                            self.go(way, source, block)
+                        return carry
+
+                    lax.fori_loop(0, self.nz * self.blocks, one, 0)
+
+    def sent(self):
+        def one(i, carry):
+            source, block = i // self.blocks, lax.rem(i, self.blocks)
+            z, y = source // self.ny, lax.rem(source, self.ny)
+            lines = [
+                jnp.logical_and(y == self.y, z <= self.z),
+                jnp.logical_and(y == self.y, z >= self.z),
+                y <= self.y,
+                y >= self.y,
+            ]
+            for way in range(4 if self.ny > 1 else 2):
+
+                @pl.when(jnp.logical_and(lines[way], self.ways[way][0]))
+                def _():
+                    self.copy(way, source, block).wait_send()
+
+            return carry
+
+        lax.fori_loop(0, self.count * self.blocks, one, 0)
+
+
+def others(count, place):
+    return [lax.rem(place + hop, count) for hop in range(1, count)]
+
+
+def greet_all(count, place):
+    barrier = pltpu.get_barrier_semaphore()
+    for peer in others(count, place):
+        pl.semaphore_signal(barrier, inc=1, device_id={"seq": peer}, device_id_type=MESH)
+    pl.semaphore_wait(barrier, count - 1)
+
+
+def start_kernel(
+    x, w, wb, stream, weights, betas, send, recv, w_send, w_recv, b_send, b_recv, own
+):
+    count, nz, ny, place, _, _ = grid_place()
+    depth = w.shape[0]
+    width = weights.shape[1] // 3
+    greet_all(count, place)
+    spread = Spread(lambda source, block: stream.at[source], 1, send, recv)
+    spread.begin(0, x)
+
+    def columns(peer, part):
+        at = pl.multiple_of((part * count + peer) * width, 128)
+        return w.at[:, pl.ds(at, width)]
+
+    def landing(source, part):
+        return weights.at[
+            pl.ds(pl.multiple_of(source * depth, 16), depth), part * width : (part + 1) * width
+        ]
+
+    def beta_copy(hop, peer, source):
+        return remote(wb, betas.at[source], b_send.at[hop], b_recv.at[hop], seq=peer)
+
+    def weight_copy(hop, peer, source, part):
+        return remote(
+            columns(peer, part), landing(source, part), w_send.at[hop, part],
+            w_recv.at[hop, part], seq=peer,
+        )
+
+    for hop, peer in enumerate(others(count, place)):
+        beta_copy(hop, peer, place).start()
+        for part in range(3):
+            weight_copy(hop, peer, place, part).start()
+    local = [
+        pltpu.make_async_copy(x, stream.at[place], own.at[0]),
+        pltpu.make_async_copy(wb, betas.at[place], own.at[1]),
+    ] + [
+        pltpu.make_async_copy(columns(place, part), landing(place, part), own.at[2 + part])
+        for part in range(3)
+    ]
+    for one in local:
+        one.start()
+    for hop in range(1, nz):
+        spread.along_z(hop, 0)
+    spread.along_y()
+    for hop, peer in enumerate(others(count, place)):
+        source = lax.rem(place + count - hop - 1, count)
+        beta_copy(hop, peer, source).wait_recv()
+        beta_copy(hop, peer, place).wait_send()
+        for part in range(3):
+            weight_copy(hop, peer, source, part).wait_recv()
+            weight_copy(hop, peer, place, part).wait_send()
+    spread.sent()
+    for one in local:
+        one.wait()
+
+
+def start_exchange(x, w, wb):
+    count = lax.axis_size("seq")
+    any_space = pl.BlockSpec(memory_space=pl.ANY)
+    dma = pltpu.SemaphoreType.DMA
+    return pl.pallas_call(
+        start_kernel,
+        out_shape=(
+            jax.ShapeDtypeStruct((count,) + x.shape, x.dtype),
+            jax.ShapeDtypeStruct((count * w.shape[0], w.shape[1] // count), w.dtype),
+            jax.ShapeDtypeStruct((count,) + wb.shape, wb.dtype),
+        ),
+        in_specs=[any_space] * 3,
+        out_specs=(any_space,) * 3,
+        scratch_shapes=[
+            dma((4, count, 1)),
+            dma((count, 1)),
+            dma((count - 1, 3)),
+            dma((count - 1, 3)),
+            dma((count - 1,)),
+            dma((count - 1,)),
+            dma((5,)),
+        ],
+        compiler_params=pltpu.CompilerParams(collective_id=0, has_side_effects=True),
+        name="start_exchange",
+    )(x, w, wb)
+
+
+def relay_kernel(blocks, out, stream, x_send, x_recv, send, recv):
+    count, nz, ny, place, _, _ = grid_place()
+    sections = lax.axis_size("section")
+    section = lax.axis_index("section")
+    after, before = lax.rem(section + 1, sections), lax.rem(section + sections - 1, sections)
+    rows = out.shape[0] // blocks
+
+    def slot(source, block):
+        at = block * rows
+        return stream.at[source, pl.ds(pl.multiple_of(at, 16), rows)]
+
+    spread = Spread(slot, blocks, send, recv)
+    barrier = pltpu.get_barrier_semaphore()
+    total = 2
+    for way, (there, peer) in enumerate(spread.neighbours()):
+        total = total + there.astype(jnp.int32)
+
+        @pl.when(there)
+        def _():
+            pl.semaphore_signal(barrier, inc=1, device_id={"seq": peer}, device_id_type=MESH)
+
+    for peer in (after, before):
+        pl.semaphore_signal(barrier, inc=1, device_id={"section": peer}, device_id_type=MESH)
+    pl.semaphore_wait(barrier, total)
+
+    def hand_on(block):
+        return remote(
+            out.at[block * rows : (block + 1) * rows], slot(place, block),
+            x_send.at[block], x_recv.at[block], section=after,
+        )
+
+    for block in range(blocks):
+        hand_on(block).start()
+    for step in range(blocks + nz - 1):
+        for block in range(blocks):
+            hop = step - block
+            if hop == 0:
+                hand_on(block).wait_recv()
+                spread.begin(block)
+            elif 0 < hop < nz:
+                spread.along_z(hop, block)
+    spread.along_y()
+    for block in range(blocks):
+        hand_on(block).wait_send()
+    spread.sent()
+
+
+def relay(out, blocks=4):
+    count = lax.axis_size("seq")
+    any_space = pl.BlockSpec(memory_space=pl.ANY)
+    dma = pltpu.SemaphoreType.DMA
+    return pl.pallas_call(
+        functools.partial(relay_kernel, blocks),
+        out_shape=jax.ShapeDtypeStruct((count,) + out.shape, out.dtype),
+        in_specs=[any_space],
+        out_specs=any_space,
+        scratch_shapes=[
+            dma((blocks,)), dma((blocks,)), dma((4, count, blocks)), dma((count, blocks)),
+        ],
+        compiler_params=pltpu.CompilerParams(collective_id=1, has_side_effects=True),
+        name="relay",
+    )(out)
+
+
+def rows_back_kernel(out, result, send, recv, own):
+    count, _, _, place, _, _ = grid_place()
+    rows, width = result.shape[0], out.shape[1]
+    greet_all(count, place)
+
+    def part(peer):
+        return out.at[pl.ds(pl.multiple_of(peer * rows, 16), rows)]
+
+    def columns(source):
+        return result.at[:, pl.ds(pl.multiple_of(source * width, 128), width)]
+
+    def copy(hop, peer, source):
+        return remote(part(peer), columns(source), send.at[hop], recv.at[hop], seq=peer)
+
+    peers = others(count, place)
+    for hop, peer in enumerate(peers):
+        copy(hop, peer, place).start()
+    mine = pltpu.make_async_copy(part(place), columns(place), own)
+    mine.start()
+    for hop, peer in enumerate(peers):
+        copy(hop, peer, lax.rem(place + count - hop - 1, count)).wait_recv()
+        copy(hop, peer, place).wait_send()
+    mine.wait()
+
+
+def rows_back(out):
+    count = lax.axis_size("seq")
+    any_space = pl.BlockSpec(memory_space=pl.ANY)
+    dma = pltpu.SemaphoreType.DMA
+    return pl.pallas_call(
+        rows_back_kernel,
+        out_shape=jax.ShapeDtypeStruct((out.shape[0] // count, out.shape[1] * count), out.dtype),
+        in_specs=[any_space],
+        out_specs=any_space,
+        scratch_shapes=[dma((count - 1,)), dma((count - 1,)), dma(())],
+        compiler_params=pltpu.CompilerParams(collective_id=2, has_side_effects=True),
+        name="rows_back",
+    )(out)
 
 
 def shards(residual, w_qkv, w_beta, beta_bias, norm_gain, out_gain, state_in, doc_start):
     count = lax.axis_size("seq")
     place = lax.axis_index("seq")
     heads = HEADS // count
-    width = heads * HD
-    depth = w_qkv.shape[1]
-    weights = jnp.concatenate(
-        [
-            w_qkv[0].reshape(depth, 3, count, width).transpose(2, 0, 1, 3).reshape(count, depth, 3 * width),
-            jnp.pad(
-                w_beta[0].reshape(depth, count, heads).transpose(1, 0, 2),
-                ((0, 0), (0, 0), (0, HD - heads)),
-            ),
-        ],
-        axis=2,
-    )
-    weights = lax.all_to_all(weights, "seq", 0, 0, tiled=True).reshape(count * depth, 3 * width + HD)
-    stream = lax.all_gather(residual[0], "seq", axis=0, tiled=True)
-    bias = lax.dynamic_slice(beta_bias, (0, place * heads), (1, heads))
-    bias = jnp.pad(bias, ((0, 0), (0, HD - heads)))
+    stream, weights, betas = start_exchange(residual[0], w_qkv[0], w_beta[0].T)
+    stream = stream.reshape(-1, stream.shape[2])
     state = lax.dynamic_slice(state_in[0], (place * heads, 0, 0), (heads, HD, HD))
     out = None
     for tick in range(TICKS):
         if tick:
-            out = lax.ppermute(
-                out, "section", [(i, (i + 1) % lax.axis_size("section")) for i in range(lax.axis_size("section"))]
-            )
-            stream = lax.all_gather(out, "seq", axis=0)
+            stream = relay(out)
         info = jnp.stack([doc_start[tick, 0], place]).astype(jnp.int32)
-        out, state = layer(stream, weights, bias, norm_gain, out_gain, state, info, heads)
-    back = lax.all_to_all(out.reshape(count, -1, width), "seq", 0, 0, tiled=True)
-    return back.transpose(1, 0, 2).reshape(1, -1, count * width)
+        out, state = layer(
+            stream, weights, betas, beta_bias, norm_gain, out_gain, state, info, heads
+        )
+    return rows_back(out)[None]
 
 
 def solution(mesh):

time: 440 us -> 357 us (0.81)
  waiting for transfers between devices: 305 us -> 0 us
  Pallas kernels: 57 us -> 345 us
  blocking collectives: 29.5 us -> 0 us
  between operations: 13.4 us -> 0.1 us
  local copies, waits for them, and re-layouts: 18.5 us -> 8.51 us
  starting transfers between devices: 6.42 us -> 0 us
    pallas_call x0 -> x3, Pallas kernels: none -> 289 us  [the longest x1 165 us: start_exchange(): pl.pallas_call(start_kernel, out_shape=(jax.ShapeDtypeStruct((count,) + x...]
    all_to_all x1 -> x0, waiting for transfers between devices: 153 us -> none  [shards(): lax.all_to_all(weights, 'seq', 0, 0, tiled=True)]
    all_gather x2 -> x0, waiting for transfers between devices: 137 us -> none  [the longest x1 122 us: shards(): stream = lax.all_gather(out, 'seq', axis=0)]
    all_to_all x1 -> x0, blocking collectives: 29.5 us -> none  [shards(): lax.all_to_all(out.reshape(count, -1, width), 'seq', 0, 0, tiled=True)]
    ppermute x1 -> x0, waiting for transfers between devices: 14.2 us -> none  [shards(): lax.ppermute(out, 'section', [(i, (i + 1) % lax.axis_size('section')) for...]
    all_to_all x1 -> x0, local copies, waits for them, and re-layouts: 6.24 us -> none  [shards(): lax.all_to_all(weights, 'seq', 0, 0, tiled=True)]
    all_to_all x1 -> x0, starting transfers between devices: 6.13 us -> none  [shards(): lax.all_to_all(weights, 'seq', 0, 0, tiled=True)]
    transpose x2 -> x0, local copies, waits for them, and re-layouts: 4.47 us -> none  [the longest x1 3.89 us: shards(): w_qkv[0].reshape(depth, 3, count, width).transpose(2, 0, 1, 3)]
  transfers between devices with their start and end apart: 4 -> 0, of which waited for: 4 -> 0; matrix products, arithmetic and copies ran while one was open for 5% -> 0% of each run, Pallas kernels for 0% -> 0%
where the time goes in v2:
time: 357 us; the launch traced here: 355 us
  Pallas kernels  345 us (97%)
  local copies, waits for them, and re-layouts  8.51 us (2%)
    pallas_call x1, Pallas kernels, start_exchange(): pl.pallas_call(start_kernel, out_shape=(jax.ShapeDtypeStruct((count,) + x...  165 us
    pallas_call x1, Pallas kernels, relay(): pl.pallas_call(functools.partial(relay_kernel, blocks), out_shape=jax.Sha...  98.2 us
    pallas_call x2, Pallas kernels, layer(): pl.pallas_call(functools.partial(layer_kernel, heads, parts), out_shape=(...  56.1 us
    pallas_call x1, Pallas kernels, rows_back(): pl.pallas_call(rows_back_kernel, out_shape=jax.ShapeDtypeStruct((out.shap...  25.7 us

profile of v2, /device:TPU:28, one launch (start us, length us, event | category | flops | bytes accessed | tf_op | source)
XLA Modules:
  0.0 355.3 jit_solution(18371028906090432519)
XLA Ops:
  0.0 0.0 copy-start
  0.0 1.4 fusion
  1.4 1.3 pad_add_fusion
  2.7 0.0 copy-done
  2.8 165.4 %start_exchange.1 = (bf16[8,256,2048]{2,1,0:T(8,128)(2,1)}, bf16[2048,768]{1,0:T(8,128)(2,1)}, bf16[8,16,256]{2,1,0:T(8,128)(2,1)}) custom-call(bf16[256,2048]{1,0:T(8,128)(2,1)} %bitcast.15, bf16[256,6144]{1,0:T(8,128)(2,1)} %bitcast.14, bf16[16,256]{1,0:T(8,128)(2,1)} %bitcast.16), custom_call_target="tpu_custom_call" | custom-call | tf_op jit(solution)/shard_map/start_exchange/pallas_call | solution.py:354
  168.1 0.0 copy-start.3
  168.1 0.8 copy-done.3
  169.0 0.0 copy-start.5
  169.0 0.7 copy-done.5
  169.7 0.0 copy-start.7
  169.7 0.7 copy-done.7
  170.3 0.0 copy-start.9
  170.3 0.7 copy-done.9
  171.0 0.0 copy-start.4
  171.0 0.0 copy-start.6
  171.0 0.0 copy-start.8
  171.0 0.0 copy-start.10
  171.0 28.3 %layer.2 = (bf16[2048,256]{1,0:T(8,128)(2,1)S(1)}, f32[2,128,128]{2,1,0:T(8,128)S(1)}) custom-call(s32[2]{0:T(128)S(1)} %get-tuple-element.20.info, bf16[2048,2048]{1,0:T(8,128)(2,1)} %bitcast.12, bf16[2048,768]{1,0:T(8,128)(2,1)} %get-tuple-element.12.w, bf16[8,16,256]{2,1,0:T(8,128)(2,1)S(1)} %copy-done.3, f32[1,16]{1,0:T(1,128)S(1)} %copy-done.7, ...), custom_call_target="tpu_custom_call" | custom-call | tf_op jit(solution)/shard_map/layer/pallas_call | solution.py:148
  199.2 0.0 copy-start.1
  199.3 1.0 copy-done.1
  200.2 98.2 %relay.1.x = bf16[8,2048,256]{2,1,0:T(8,128)(2,1)} custom-call(bf16[2048,256]{1,0:T(8,128)(2,1)} %copy-done.1), custom_call_target="tpu_custom_call" | custom-call | tf_op jit(solution)/shard_map/relay/pallas_call | solution.py:428
  298.4 0.0 copy-done.4
  298.4 0.0 copy-done.6
  298.4 0.0 copy-done.8
  298.4 0.0 copy-done.10
  298.4 27.9 %layer.3 = (bf16[2048,256]{1,0:T(8,128)(2,1)S(1)}, f32[2,128,128]{2,1,0:T(8,128)}) custom-call(s32[2]{0:T(128)S(1)} %get-tuple-element.19.info, bf16[8,2048,256]{2,1,0:T(8,128)(2,1)} %relay.1.x, bf16[2048,768]{1,0:T(8,128)(2,1)} %get-tuple-element.12.w, bf16[8,16,256]{2,1,0:T(8,128)(2,1)S(1)} %copy-done.4, f32[1,16]{1,0:T(1,128)S(1)} %copy-done.8, ...), custom_call_target="tpu_custom_call" | custom-call | tf_op jit(solution)/shard_map/layer/pallas_call | solution.py:148
  326.3 0.0 copy-start.2
  326.3 1.0 copy-done.2
  327.3 25.7 %rows_back.1 = bf16[256,2048]{1,0:T(8,128)(2,1)} custom-call(bf16[2048,256]{1,0:T(8,128)(2,1)} %copy-done.2), custom_call_target="tpu_custom_call" | custom-call | tf_op jit(solution)/shard_map/rows_back/pallas_call | solution.py:470
  353.0 2.3 copy.10
  (1 shorter events, 0.0 us)
Async XLA Ops:
  0.0 2.7 copy-start
  168.1 0.8 copy-start.3
  169.0 0.7 copy-start.5
  169.7 0.7 copy-start.7
  170.3 0.7 copy-start.9
  171.0 127.4 %copy-start.4 = (bf16[8,16,256]{2,1,0:T(8,128)(2,1)S(1)}, bf16[8,16,256]{2,1,0:T(8,128)(2,1)}, u32[]{:S(2)}) copy-start(bf16[8,16,256]{2,1,0:T(8,128)(2,1)} %get-tuple-element.13.wb) | copy-start | bytes 196612
  171.0 127.4 %copy-start.6 = (f32[1,2048]{1,0:T(1,128)S(1)}, f32[1,2048]{1,0:T(1,128)}, u32[]{:S(2)}) copy-start(f32[1,2048]{1,0:T(1,128)} %in_gain.3) | copy-start | bytes 24580
  171.0 127.4 %copy-start.8 = (f32[1,16]{1,0:T(1,128)S(1)}, f32[1,16]{1,0:T(1,128)}, u32[]{:S(2)}) copy-start(f32[1,16]{1,0:T(1,128)} %bias.3) | copy-start | bytes 196
  171.0 127.4 %copy-start.10 = (f32[1,128]{1,0:T(1,128)S(1)}, f32[1,128]{1,0:T(1,128)}, u32[]{:S(2)}) copy-start(f32[1,128]{1,0:T(1,128)} %out_gain.3) | copy-start | bytes 1540
  199.2 1.0 copy-start.1
  326.3 1.0 copy-start.2

commit v3 on v2

--- a/solution.py
+++ b/solution.py
@@ -107,72 +107,6 @@
     return (residual.astype(F32) + mixed).astype(BF16)
 
 
-def layer_kernel(heads, parts, info, x, w, wb, bias, in_gain, out_gain, entry, out, final):
-    step = pl.program_id(0)
-    width = heads * HD
-
-    @pl.when(step == 0)
-    def _():
-        final[...] = entry[...]
-
-    if parts:
-        wide = jnp.concatenate([x[c] for c in range(parts)], axis=1).astype(F32)
-        residual = x[info[1]]
-    else:
-        wide = x[...].astype(F32)
-        residual = x[:, pl.ds(pl.multiple_of(info[1] * width, HD), width)]
-    normed = wide * lax.rsqrt(jnp.mean(wide * wide, axis=-1, keepdims=True) + 1e-05) * in_gain[...]
-    rows = wide.shape[0]
-    state = [final[h] for h in range(heads)]
-    out[...] = layer_rows(
-        normed.astype(BF16), w[...],
-        jnp.concatenate([wb[c] for c in range(wb.shape[0])], axis=1),
-        bias[...], out_gain[...], residual, state, heads, info[1] * heads, info[0], step * (rows // GROUP),
-    )
-    for h in range(heads):
-        final[h] = state[h]
-
-
-def layer(x, w, wb, bias, in_gain, out_gain, entry, info, heads, rows=512):
-    parts = x.shape[0] if x.ndim == 3 else 0
-    total, d = x.shape[-2], in_gain.shape[-1]
-    width = heads * HD
-    if parts:
-        x_spec = pl.BlockSpec((parts, rows, x.shape[2]), lambda i, s: (0, i, 0))
-    else:
-        x_spec = pl.BlockSpec((rows, d), lambda i, s: (i, 0))
-
-    def whole(shape):
-        return pl.BlockSpec(shape, lambda i, s: (0,) * len(shape))
-
-    return pl.pallas_call(
-        functools.partial(layer_kernel, heads, parts),
-        out_shape=(
-            jax.ShapeDtypeStruct((total, width), BF16),
-            jax.ShapeDtypeStruct((heads, HD, HD), F32),
-        ),
-        grid_spec=pltpu.PrefetchScalarGridSpec(
-            num_scalar_prefetch=1,
-            grid=(total // rows,),
-            in_specs=[
-                x_spec,
-                whole(w.shape),
-                whole(wb.shape),
-                whole(bias.shape),
-                whole(in_gain.shape),
-                whole(out_gain.shape),
-                whole(entry.shape),
-            ],
-            out_specs=(
-                pl.BlockSpec((rows, width), lambda i, s: (i, 0)),
-                whole((heads, HD, HD)),
-            ),
-        ),
-        compiler_params=pltpu.CompilerParams(vmem_limit_bytes=50 * 2**20),
-        name="layer",
-    )(info, x, w, wb, bias, in_gain, out_gain, entry)
-
-
 MESH = pl.DeviceIdType.MESH
 Z_CHIPS = 4
 
@@ -243,21 +177,17 @@
                 self.go(2, source, block)
                 self.go(3, source, block)
 
-    def along_y(self):
+    def along_y(self, block):
         for hop in range(1, self.ny):
             for way, sign in ((2, -1), (3, 1)):
                 y = self.y + sign * hop
 
                 @pl.when(jnp.logical_and(y >= 0, y < self.ny))
                 def _():
-                    def one(i, carry):
-                        source, block = (i // self.blocks) * self.ny + y, lax.rem(i, self.blocks)
-                        self.arrived(source, block)
+                    for z in range(self.nz):
+                        self.arrived(z * self.ny + y, block)
                         if hop + 1 < self.ny:
-                            self.go(way, source, block)
-                        return carry
-
-                    lax.fori_loop(0, self.nz * self.blocks, one, 0)
+                            self.go(way, z * self.ny + y, block)
 
     def sent(self):
         def one(i, carry):
@@ -334,7 +264,7 @@
         one.start()
     for hop in range(1, nz):
         spread.along_z(hop, 0)
-    spread.along_y()
+    spread.along_y(0)
     for hop, peer in enumerate(others(count, place)):
         source = lax.rem(place + count - hop - 1, count)
         beta_copy(hop, peer, source).wait_recv()
@@ -374,108 +304,144 @@
     )(x, w, wb)
 
 
-def relay_kernel(blocks, out, stream, x_send, x_recv, send, recv):
+def ticks_kernel(
+    blocks, doc, x, w, wb, bias, in_gain, out_gain, entry, result,
+    stream, outs, state, x_send, x_recv, send, recv, back_send, back_recv, own,
+):
     count, nz, ny, place, _, _ = grid_place()
     sections = lax.axis_size("section")
     section = lax.axis_index("section")
     after, before = lax.rem(section + 1, sections), lax.rem(section + sections - 1, sections)
-    rows = out.shape[0] // blocks
+    heads = HEADS // count
+    width = heads * HD
+    rows = x.shape[0] // blocks
+    share = x.shape[0] // count
+
+    def at(block, size):
+        return pl.ds(pl.multiple_of(block * size, 16), size)
 
     def slot(source, block):
-        at = block * rows
-        return stream.at[source, pl.ds(pl.multiple_of(at, 16), rows)]
+        return stream.at[source, at(block, rows)]
 
     spread = Spread(slot, blocks, send, recv)
     barrier = pltpu.get_barrier_semaphore()
-    total = 2
-    for way, (there, peer) in enumerate(spread.neighbours()):
-        total = total + there.astype(jnp.int32)
-
-        @pl.when(there)
-        def _():
-            pl.semaphore_signal(barrier, inc=1, device_id={"seq": peer}, device_id_type=MESH)
-
+    for peer in others(count, place):
+        pl.semaphore_signal(barrier, inc=1, device_id={"seq": peer}, device_id_type=MESH)
     for peer in (after, before):
         pl.semaphore_signal(barrier, inc=1, device_id={"section": peer}, device_id_type=MESH)
-    pl.semaphore_wait(barrier, total)
+    pl.semaphore_wait(barrier, count + 1)
 
     def hand_on(block):
         return remote(
-            out.at[block * rows : (block + 1) * rows], slot(place, block),
+            outs.at[0, at(block, rows)], slot(place, block),
             x_send.at[block], x_recv.at[block], section=after,
         )
 
-    for block in range(blocks):
-        hand_on(block).start()
-    for step in range(blocks + nz - 1):
-        for block in range(blocks):
-            hop = step - block
-            if hop == 0:
-                hand_on(block).wait_recv()
-                spread.begin(block)
-            elif 0 < hop < nz:
-                spread.along_z(hop, block)
-    spread.along_y()
+    def columns(source):
+        return result.at[:, pl.ds(pl.multiple_of(source * width, 128), width)]
+
+    def back(peer, source):
+        return remote(
+            outs.at[1, at(peer, share)], columns(source),
+            back_send.at[peer], back_recv.at[source], seq=peer,
+        )
+
+    def keep_own():
+        return pltpu.make_async_copy(outs.at[1, at(place, share)], columns(place), own)
+
+    def compute(tick, block, wide, residual):
+        wide = wide.astype(F32)
+        scale = lax.rsqrt(jnp.mean(wide * wide, axis=-1, keepdims=True) + 1e-05)
+        normed = (wide * scale * in_gain[...]).astype(BF16)
+        now = [state[h] for h in range(heads)]
+        outs[tick, at(block, rows)] = layer_rows(
+            normed, w[...], jnp.concatenate([wb[c] for c in range(count)], axis=1), bias[...],
+            out_gain[...], residual, now, heads, place * heads, doc[tick], block * (rows // GROUP),
+        )
+        for h in range(heads):
+            state[h] = now[h]
+
+    state[...] = entry[...]
+
+    def step(u, carry):
+        @pl.when(u < blocks)
+        def _():
+            here = at(u, rows)
+            mine = pl.ds(pl.multiple_of(place * width, 128), width)
+            compute(0, u, x[here, :], x[here, mine])
+            hand_on(u).start()
+
+        for hop in range(nz):
+            block = u - 1 - hop
+
+            @pl.when(jnp.logical_and(block >= 0, block < blocks))
+            def _():
+                if hop == 0:
+                    hand_on(block).wait_recv()
+                    spread.begin(block)
+                else:
+                    spread.along_z(hop, block)
+
+        ready = u - nz - 1
+
+        @pl.when(ready >= 0)
+        def _():
+            spread.along_y(ready)
+            here = at(ready, rows)
+            wide = jnp.concatenate([stream[c, here] for c in range(count)], axis=1)
+            compute(1, ready, wide, stream[place, here])
+            for i in range(rows // share):
+                peer = ready * (rows // share) + i
+
+                @pl.when(peer != place)
+                def _():
+                    back(peer, place).start()
+
+                @pl.when(peer == place)
+                def _():
+                    keep_own().start()
+
+        return carry
+
+    lax.fori_loop(0, blocks + nz + 1, step, 0)
     for block in range(blocks):
         hand_on(block).wait_send()
     spread.sent()
-
-
-def relay(out, blocks=4):
+    for peer in others(count, place):
+        back(peer, place).wait_send()
+        back(place, peer).wait_recv()
+    keep_own().wait()
+
+
+def ticks(doc, x, w, wb, bias, in_gain, out_gain, entry, blocks=4):
     count = lax.axis_size("seq")
-    any_space = pl.BlockSpec(memory_space=pl.ANY)
+    heads = entry.shape[0]
+    width = heads * HD
+    total, d = x.shape
     dma = pltpu.SemaphoreType.DMA
+    vmem = pl.BlockSpec(memory_space=pltpu.VMEM)
     return pl.pallas_call(
-        functools.partial(relay_kernel, blocks),
-        out_shape=jax.ShapeDtypeStruct((count,) + out.shape, out.dtype),
-        in_specs=[any_space],
-        out_specs=any_space,
+        functools.partial(ticks_kernel, blocks),
+        out_shape=jax.ShapeDtypeStruct((total // count, d), BF16),
+        in_specs=[pl.BlockSpec(memory_space=pltpu.SMEM)] + [vmem] * 7,
+        out_specs=pl.BlockSpec(memory_space=pl.ANY),
         scratch_shapes=[
-            dma((blocks,)), dma((blocks,)), dma((4, count, blocks)), dma((count, blocks)),
+            pltpu.VMEM((count, total, width), BF16),
+            pltpu.VMEM((TICKS, total, width), BF16),
+            pltpu.VMEM((heads, HD, HD), F32),
+            dma((blocks,)),
+            dma((blocks,)),
+            dma((4, count, blocks)),
+            dma((count, blocks)),
+            dma((count,)),
+            dma((count,)),
+            dma(()),
         ],
-        compiler_params=pltpu.CompilerParams(collective_id=1, has_side_effects=True),
-        name="relay",
-    )(out)
-
-
-def rows_back_kernel(out, result, send, recv, own):
-    count, _, _, place, _, _ = grid_place()
-    rows, width = result.shape[0], out.shape[1]
-    greet_all(count, place)
-
-    def part(peer):
-        return out.at[pl.ds(pl.multiple_of(peer * rows, 16), rows)]
-
-    def columns(source):
-        return result.at[:, pl.ds(pl.multiple_of(source * width, 128), width)]
-
-    def copy(hop, peer, source):
-        return remote(part(peer), columns(source), send.at[hop], recv.at[hop], seq=peer)
-
-    peers = others(count, place)
-    for hop, peer in enumerate(peers):
-        copy(hop, peer, place).start()
-    mine = pltpu.make_async_copy(part(place), columns(place), own)
-    mine.start()
-    for hop, peer in enumerate(peers):
-        copy(hop, peer, lax.rem(place + count - hop - 1, count)).wait_recv()
-        copy(hop, peer, place).wait_send()
-    mine.wait()
-
-
-def rows_back(out):
-    count = lax.axis_size("seq")
-    any_space = pl.BlockSpec(memory_space=pl.ANY)
-    dma = pltpu.SemaphoreType.DMA
-    return pl.pallas_call(
-        rows_back_kernel,
-        out_shape=jax.ShapeDtypeStruct((out.shape[0] // count, out.shape[1] * count), out.dtype),
-        in_specs=[any_space],
-        out_specs=any_space,
-        scratch_shapes=[dma((count - 1,)), dma((count - 1,)), dma(())],
-        compiler_params=pltpu.CompilerParams(collective_id=2, has_side_effects=True),
-        name="rows_back",
-    )(out)
+        compiler_params=pltpu.CompilerParams(
+            collective_id=1, has_side_effects=True, vmem_limit_bytes=58 * 2**20
+        ),
+        name="ticks",
+    )(doc, x, w, wb, bias, in_gain, out_gain, entry)
 
 
 def shards(residual, w_qkv, w_beta, beta_bias, norm_gain, out_gain, state_in, doc_start):
@@ -485,15 +451,10 @@
     stream, weights, betas = start_exchange(residual[0], w_qkv[0], w_beta[0].T)
     stream = stream.reshape(-1, stream.shape[2])
     state = lax.dynamic_slice(state_in[0], (place * heads, 0, 0), (heads, HD, HD))
-    out = None
-    for tick in range(TICKS):
-        if tick:
-            stream = relay(out)
-        info = jnp.stack([doc_start[tick, 0], place]).astype(jnp.int32)
-        out, state = layer(
-            stream, weights, betas, beta_bias, norm_gain, out_gain, state, info, heads
-        )
-    return rows_back(out)[None]
+    out = ticks(
+        doc_start[:, 0], stream, weights, betas, beta_bias, norm_gain, out_gain, state
+    )
+    return out[None]
 
 
 def solution(mesh):

time: 357 us -> 312 us (0.87)
  Pallas kernels: 345 us -> 308 us
  local copies, waits for them, and re-layouts: 8.51 us -> 4.19 us
    pallas_call x4 -> x1, Pallas kernels: 180 us -> 143 us  [ticks(): pl.pallas_call(functools.partial(ticks_kernel, blocks), out_shape=jax.Sha...]
where the time goes in v3:
time: 312 us
  Pallas kernels  308 us (99%)
  local copies, waits for them, and re-layouts  4.19 us (1%)
    pallas_call x1, Pallas kernels, start_exchange(): pl.pallas_call(start_kernel, out_shape=(jax.ShapeDtypeStruct((count,) + x...  165 us
    pallas_call x1, Pallas kernels, ticks(): pl.pallas_call(functools.partial(ticks_kernel, blocks), out_shape=jax.Sha...  143 us

profile of v3, /device:TPU:28, one launch (start us, length us, event | category | flops | bytes accessed | tf_op | source)
XLA Modules:
  0.0 312.0 jit_solution(13103136574303623224)
XLA Ops:
  0.0 0.0 copy-start
  0.0 1.2 copy-done
  1.2 0.7 dynamic-slice_bitcast_fusion.entry
  1.9 165.3 %start_exchange.1 = (bf16[8,256,2048]{2,1,0:T(8,128)(2,1)}, bf16[2048,768]{1,0:T(8,128)(2,1)}, bf16[8,16,256]{2,1,0:T(8,128)(2,1)}) custom-call(bf16[256,2048]{1,0:T(8,128)(2,1)} %bitcast.13, bf16[256,6144]{1,0:T(8,128)(2,1)} %bitcast.12, bf16[16,256]{1,0:T(8,128)(2,1)} %bitcast.14), custom_call_target="tpu_custom_call" | custom-call | tf_op jit(solution)/shard_map/start_exchange/pallas_call | solution.py:284
  167.2 142.5 %ticks.1 = bf16[256,2048]{1,0:T(8,128)(2,1)} custom-call(s32[2]{0:T(128)} %bitcast.15, bf16[2048,2048]{1,0:T(8,128)(2,1)} %bitcast.10, bf16[2048,768]{1,0:T(8,128)(2,1)} %get-tuple-element.9.w, bf16[8,16,256]{2,1,0:T(8,128)(2,1)} %get-tuple-element.10.wb, f32[1,16]{1,0:T(1,128)} %bias.1, f32[1,2048]{1,0:T(1,128)} %in_gain.1, f32[1,128]{1,0:T(1,128)} %out_gain.1, ...), custom_call_target="tpu_custom_call" | custom-call | tf_op jit(solution)/shard_map/ticks/pallas_call | solution.py:423
  309.7 2.3 copy.10
Async XLA Ops:
  0.0 1.2 copy-start

commit v4 on v3

--- a/solution.py
+++ b/solution.py
@@ -222,14 +222,20 @@
 
 
 def start_kernel(
-    x, w, wb, stream, weights, betas, send, recv, w_send, w_recv, b_send, b_recv, own
+    blocks, x, w, wb, stream, weights, betas, send, recv, w_send, w_recv, b_send, b_recv, own
 ):
     count, nz, ny, place, _, _ = grid_place()
     depth = w.shape[0]
     width = weights.shape[1] // 3
     greet_all(count, place)
-    spread = Spread(lambda source, block: stream.at[source], 1, send, recv)
-    spread.begin(0, x)
+    rows = x.shape[0] // blocks
+
+    def piece(block):
+        return pl.ds(pl.multiple_of(block * rows, 16), rows)
+
+    spread = Spread(lambda source, block: stream.at[source, piece(block)], blocks, send, recv)
+    for block in range(blocks):
+        spread.begin(block, x.at[piece(block)])
 
     def columns(peer, part):
         at = pl.multiple_of((part * count + peer) * width, 128)
@@ -263,8 +269,10 @@
     for one in local:
         one.start()
     for hop in range(1, nz):
-        spread.along_z(hop, 0)
-    spread.along_y(0)
+        for block in range(blocks):
+            spread.along_z(hop, block)
+    for block in range(blocks):
+        spread.along_y(block)
     for hop, peer in enumerate(others(count, place)):
         source = lax.rem(place + count - hop - 1, count)
         beta_copy(hop, peer, source).wait_recv()
@@ -277,12 +285,12 @@
         one.wait()
 
 
-def start_exchange(x, w, wb):
+def start_exchange(x, w, wb, blocks=4):
     count = lax.axis_size("seq")
     any_space = pl.BlockSpec(memory_space=pl.ANY)
     dma = pltpu.SemaphoreType.DMA
     return pl.pallas_call(
-        start_kernel,
+        functools.partial(start_kernel, blocks),
         out_shape=(
             jax.ShapeDtypeStruct((count,) + x.shape, x.dtype),
             jax.ShapeDtypeStruct((count * w.shape[0], w.shape[1] // count), w.dtype),
@@ -291,8 +299,8 @@
         in_specs=[any_space] * 3,
         out_specs=(any_space,) * 3,
         scratch_shapes=[
-            dma((4, count, 1)),
-            dma((count, 1)),
+            dma((4, count, blocks)),
+            dma((count, blocks)),
             dma((count - 1, 3)),
             dma((count - 1, 3)),
             dma((count - 1,)),

time: 312 us -> 281 us (0.901)
  Pallas kernels: 308 us -> 277 us
    pallas_call x1, Pallas kernels: 165 us -> 134 us  [start_exchange(): pl.pallas_call(functools.partial(start_kernel, blocks), out_shape=(jax.Sh...]
where the time goes in v4:
time: 281 us
  Pallas kernels  277 us (99%)
  local copies, waits for them, and re-layouts  4.19 us (1%)
    pallas_call x1, Pallas kernels, ticks(): pl.pallas_call(functools.partial(ticks_kernel, blocks), out_shape=jax.Sha...  143 us
    pallas_call x1, Pallas kernels, start_exchange(): pl.pallas_call(functools.partial(start_kernel, blocks), out_shape=(jax.Sh...  134 us

profile of v4, /device:TPU:28, one launch (start us, length us, event | category | flops | bytes accessed | tf_op | source)
XLA Modules:
  0.0 280.8 jit_solution(16645947947403962211)
XLA Ops:
  0.0 0.0 copy-start
  0.0 1.2 copy-done
  1.2 0.7 dynamic-slice_bitcast_fusion.entry
  1.9 133.6 %start_exchange.1 = (bf16[8,256,2048]{2,1,0:T(8,128)(2,1)}, bf16[2048,768]{1,0:T(8,128)(2,1)}, bf16[8,16,256]{2,1,0:T(8,128)(2,1)}) custom-call(bf16[256,2048]{1,0:T(8,128)(2,1)} %bitcast.13, bf16[256,6144]{1,0:T(8,128)(2,1)} %bitcast.12, bf16[16,256]{1,0:T(8,128)(2,1)} %bitcast.14), custom_call_target="tpu_custom_call" | custom-call | tf_op jit(solution)/shard_map/start_exchange/pallas_call | solution.py:292
  135.5 143.0 %ticks.1 = bf16[256,2048]{1,0:T(8,128)(2,1)} custom-call(s32[2]{0:T(128)} %bitcast.15, bf16[2048,2048]{1,0:T(8,128)(2,1)} %bitcast.10, bf16[2048,768]{1,0:T(8,128)(2,1)} %get-tuple-element.9.w, bf16[8,16,256]{2,1,0:T(8,128)(2,1)} %get-tuple-element.10.wb, f32[1,16]{1,0:T(1,128)} %bias.1, f32[1,2048]{1,0:T(1,128)} %in_gain.1, f32[1,128]{1,0:T(1,128)} %out_gain.1, ...), custom_call_target="tpu_custom_call" | custom-call | tf_op jit(solution)/shard_map/ticks/pallas_call | solution.py:431
  278.5 2.3 copy.10
Async XLA Ops:
  0.0 1.2 copy-start
